TPU v7x, 512 devices: a whole 4x8x8 slice. The times are simulated.
512 devices in a mesh: dp: 64 (over y, x, core), fsdp: 8 (over z).
Axes of the slice: x: 4, y: 8, z: 8, core: 2. Of those that a mesh axis runs over, the one named last changes fastest.
Arguments:
- queries: bfloat16 [65536, 3584], P(('dp', 'fsdp')), may hold values from -60 to 60
- keys: bfloat16 [65536, 512], P(('dp', 'fsdp')), may hold values from -6 to 6
- values: bfloat16 [65536, 512], P(('dp', 'fsdp')), may hold values from -6 to 6
- out_grad: bfloat16 [65536, 3584], P(('dp', 'fsdp')), may hold values from -6 to 6
- doc_first: int32 [512, 2], replicated, may hold values from 0 to 1, as said below
- doc_valid: int32 [512, 2], replicated, may hold values from 1 to 64
- move_plan: int32 [3, 512, 2], replicated, may hold values from 0 to 1, as said below
Outputs:
- attended: bfloat16 [65536, 3584], P(('dp', 'fsdp'))
- query_grad: bfloat16 [65536, 3584], P(('dp', 'fsdp'))
- key_grad: bfloat16 [65536, 512], P(('dp', 'fsdp'))
- value_grad: bfloat16 [65536, 512], P(('dp', 'fsdp'))
Inputs may be any that keep to these rules, and one draw needn't show every extreme that they name: `doc_first`: block 0 of every micro-batch begins a document; a document covers the blocks from its first block up to the next document's first block; all its blocks but the last have 64 live rows. `move_plan`: A flag is equal for a micro-batch and its partner of the section; the flagged blocks of a micro-batch at a section never include block 0 and form a suffix that starts a document in both micro-batches as they stand at that section.
All inputs are finite; a program needn't handle non-finite values.
Results may differ from a plain program's by a relative error of at most 0.013.
Values may be sent and summed in bfloat16 or wider, within the bound.
No kernel may reach another device: no remote copies, remote signals or barrier semaphores. Data moves between devices by JAX's collectives and lax.ppermute only.
A program may use at most 64 MiB of HBM per device.

v0:
```python
import jax
import jax.numpy as jnp
from jax import lax
from jax.sharding import PartitionSpec as P

KVH = 4
GROUP = 7
BLOCKS = 2


def partner_2(shard, axis, bit):
    return lax.ppermute(shard, axis, [(i, i ^ 1 << bit) for i in range(lax.axis_size(axis))])


def attend_local(query_rows, key_rows, value_rows, grad_rows, allow):
    head_size = key_rows.shape[1] // KVH
    scale = 1.0 / head_size**0.5
    count = query_rows.shape[0]
    outs, dqs, dks, dvs = ([], [], [], [])
    for head_idx in range(KVH):
        lower = head_idx * GROUP * head_size
        qh = query_rows[:, lower : lower + GROUP * head_size].reshape(count, GROUP, head_size)
        dh = grad_rows[:, lower : lower + GROUP * head_size].reshape(count, GROUP, head_size)
        kh = key_rows[:, head_idx * head_size : (head_idx + 1) * head_size]
        vh = value_rows[:, head_idx * head_size : (head_idx + 1) * head_size]
        score = jnp.einsum("rgd,sd->grs", qh, kh, preferred_element_type=jnp.float32) * scale
        masked = jnp.where(allow[None], score, -1e30)
        top = jnp.max(masked, axis=-1, keepdims=True)
        weights = jnp.exp(masked - top)
        probs = weights / jnp.sum(weights, axis=-1, keepdims=True)
        probs_b = probs.astype(jnp.bfloat16)
        outs.append(
            jnp.einsum("grs,sd->rgd", probs_b, vh, preferred_element_type=jnp.float32)
            .astype(jnp.bfloat16)
            .reshape(count, GROUP * head_size)
        )
        dprob = jnp.einsum("rgd,sd->grs", dh, vh, preferred_element_type=jnp.float32)
        delta = jnp.sum(probs * dprob, axis=-1, keepdims=True)
        dscore = (probs * (dprob - delta) * scale).astype(jnp.bfloat16)
        dqs.append(
            jnp.einsum("grs,sd->rgd", dscore, kh, preferred_element_type=jnp.float32)
            .astype(jnp.bfloat16)
            .reshape(count, GROUP * head_size)
        )
        dks.append(jnp.einsum("grs,rgd->sd", dscore, qh, preferred_element_type=jnp.float32))
        dvs.append(jnp.einsum("grs,rgd->sd", probs_b, dh, preferred_element_type=jnp.float32))
    return (
        jnp.concatenate(outs, 1),
        jnp.concatenate(dqs, 1),
        jnp.concatenate(dks, 1),
        jnp.concatenate(dvs, 1),
    )


def tile_terms(query_rows, key_rows, value_rows, grad_rows, first_row, valid_row, block_rows):
    query_pos = jnp.arange(query_rows.shape[0], dtype=jnp.int32)
    key_pos = jnp.arange(key_rows.shape[0], dtype=jnp.int32)
    starting = first_row[query_pos // block_rows] * block_rows
    living = key_pos % block_rows < valid_row[key_pos // block_rows]
    allow = (
        (key_pos[None, :] >= starting[:, None])
        & (key_pos[None, :] <= query_pos[:, None])
        & living[None, :]
    )
    return attend_local(query_rows, key_rows, value_rows, grad_rows, allow)


def compute(query_rows, key_rows, value_rows, grad_rows, first_row, valid_row):
    total_rows = query_rows.shape[0]
    block_rows = total_rows // BLOCKS
    out, dq, dk_total, dv_total = tile_terms(
        query_rows, key_rows, value_rows, grad_rows, first_row, valid_row, block_rows
    )
    return (out, dq, dk_total.astype(jnp.bfloat16), dv_total.astype(jnp.bfloat16))


def body(queries, keys, values, out_grad, doc_first, doc_valid, move_plan):
    near_count = lax.axis_size("fsdp")
    micro_id = lax.axis_index("dp") * near_count + lax.axis_index("fsdp")
    total_rows = queries.shape[0]
    block_rows = total_rows // BLOCKS
    section_count = move_plan.shape[0]
    near_bits = near_count.bit_length() - 1
    far_top = lax.axis_size("dp").bit_length() - 2
    micro_ids = jnp.arange(doc_first.shape[0], dtype=jnp.int32)
    moved_first = doc_first
    moved_valid = doc_valid
    for section_idx in range(section_count):
        if section_idx == 0:
            shift_bits = 0
        elif section_idx == 1:
            shift_bits = near_bits
        else:
            shift_bits = near_bits + far_top
        partner = jnp.bitwise_xor(micro_ids, 1 << shift_bits)
        moved_first = jnp.where(move_plan[section_idx] == 1, moved_first[partner], moved_first)
        moved_valid = jnp.where(move_plan[section_idx] == 1, moved_valid[partner], moved_valid)
    out, dq, dk, dv = compute(
        queries, keys, values, out_grad, doc_first[micro_id], doc_valid[micro_id]
    )
    current = (out, dq, dk, dv)
    for section_idx in range(section_count):
        row_flags = jnp.repeat(move_plan[section_idx, micro_id], block_rows) == 1
        sent = current
        if section_idx == 0:
            incoming = partner_2((sent[0], sent[1], sent[2], sent[3]), "fsdp", 0)
        else:
            far_bit = 0 if section_idx == 1 else far_top
            incoming = partner_2((sent[0], sent[1], sent[2], sent[3]), "dp", far_bit)
        merged = tuple(
            (jnp.where(row_flags[:, None], got, own) for got, own in zip(incoming, sent))
        )
        current = merged
    out, dq, dk, dv = current
    return (out, dq, dk, dv)


def solution(mesh):
    placed = (
        P(("dp", "fsdp"), None),
        P(("dp", "fsdp"), None),
        P(("dp", "fsdp"), None),
        P(("dp", "fsdp"), None),
        P(),
        P(),
        P(),
    )
    return jax.shard_map(
        body,
        mesh=mesh,
        in_specs=placed,
        out_specs=(
            P(("dp", "fsdp"), None),
            P(("dp", "fsdp"), None),
            P(("dp", "fsdp"), None),
            P(("dp", "fsdp"), None),
        ),
        check_vma=False,
    )
```

profile of v0, /device:TPU:436, one launch (start us, length us, event | category | flops | bytes accessed | tf_op | source)
XLA Modules:
  0.0 187.5 jit_solution(14404971707478810244)
XLA Ops:
  0.6 0.8 constant_dynamic-slice_fusion
  1.4 0.5 fusion.196
  1.9 0.5 fusion.197
  2.4 1.4 fusion.195
  3.8 0.2 copy.152
  4.0 0.2 copy.156
  4.2 0.2 copy.154
  4.4 0.2 copy.158
  4.6 1.3 fusion.130
  5.9 1.3 fusion.133
  7.3 1.1 fusion.198
  8.4 1.1 fusion.204
  9.4 1.1 fusion.201
  10.5 1.1 fusion.207
  11.8 0.6 copy-done.23
  12.5 0.2 convolution_bitcast_fusion.3
  12.7 1.6 convolution_convert_fusion.7
  14.5 0.2 copy.161
  14.7 0.2 convolution_bitcast_fusion.1
  14.9 1.6 convolution_convert_fusion.5
  16.7 0.2 copy.160
  16.9 0.2 convolution_bitcast_fusion.2
  17.1 1.6 convolution_convert_fusion.6
  18.9 0.2 copy.162
  19.1 0.2 convolution_bitcast_fusion
  19.4 1.6 convolution_convert_fusion.4
  21.3 3.4 %collective-permute-start.3 = (bf16[128,3584]{1,0:T(8,128)(2,1)S(1)}, bf16[128,3584]{1,0:T(8,128)(2,1)}, u32[]{:S(2)}, u32[]{:S(2)}) collective-permute-start(bf16[128,3584]{1,0:T(8,128)(2,1)S(1)} %pad_maximum_fusion.1), channel_id=1, source_target_pairs={{0,1},{1,0},{2,3},{3,2},{4,5},{5,4},{6,7},{7,6},{8,9},{9,8},{10,11... | collective-permute-start | bytes 2752520 | tf_op jit(solution)/shard_map/ppermute | solution.py:12
  24.7 1.9 %convolution_convert_fusion = bf16[7,128,128]{1,2,0:T(8,128)(2,1)} fusion(bf16[128,512]{1,0:T(8,128)(2,1)S(1)} %copy-done.24, f32[7,128]{1,0:T(8,128)S(1)} %get-tuple-element.39, bf16[128,7,128]{0,2,1:T(8,128)(2,1)S(1)} %bitcast.299, pred[128,128]{0,1:T(8,128)(4,1)S(1)} %fusion.81, bf16[128,512]{1,0:T(8,128)(2,1)} %param.8), kind=kOutput, calls=%fused_computation.48 | convolution fusion | flops 59409408 | bytes 544768 | tf_op jit(solution)/shard_map/grs,sd->rgd/dot_general | solution.py:33
  26.6 1.9 %convolution_convert_fusion.2 = bf16[7,128,128]{1,2,0:T(8,128)(2,1)} fusion(bf16[128,512]{1,0:T(8,128)(2,1)S(1)} %copy-done.24, f32[7,128]{1,0:T(8,128)S(1)} %get-tuple-element.43, bf16[128,7,128]{0,2,1:T(8,128)(2,1)S(1)} %bitcast.303, pred[128,128]{0,1:T(8,128)(4,1)S(1)} %fusion.81, bf16[128,512]{1,0:T(8,128)(2,1)} %param.8), kind=kOutput, calls=%fused_computation.50 | convolution fusion | flops 59409408 | bytes 544768 | tf_op jit(solution)/shard_map/grs,sd->rgd/dot_general | solution.py:33
  28.5 1.9 %convolution_convert_fusion.1 = bf16[7,128,128]{1,2,0:T(8,128)(2,1)} fusion(bf16[128,512]{1,0:T(8,128)(2,1)S(1)} %copy-done.24, f32[7,128]{1,0:T(8,128)S(1)} %get-tuple-element.41, bf16[128,7,128]{0,2,1:T(8,128)(2,1)S(1)} %bitcast.307, pred[128,128]{0,1:T(8,128)(4,1)S(1)} %fusion.81, bf16[128,512]{1,0:T(8,128)(2,1)} %param.8), kind=kOutput, calls=%fused_computation.49 | convolution fusion | flops 59409408 | bytes 544768 | tf_op jit(solution)/shard_map/grs,sd->rgd/dot_general | solution.py:33
  30.4 1.3 convolution_convert_fusion.3
  32.1 0.6 copy-done.20
  33.0 1.0 pad_maximum_fusion
  34.0 2.4 %collective-permute-start = (bf16[128,3584]{1,0:T(8,128)(2,1)}, bf16[128,3584]{1,0:T(8,128)(2,1)}, u32[]{:S(2)}, u32[]{:S(2)}) collective-permute-start(bf16[128,3584]{1,0:T(8,128)(2,1)} %pad_maximum_fusion), channel_id=1, source_target_pairs={{0,1},{1,0},{2,3},{3,2},{4,5},{5,4},{6,7},{7,6},{8,9},{9,8},{10,11... | collective-permute-start | bytes 2752520 | tf_op jit(solution)/shard_map/ppermute | solution.py:12
  36.5 1.4 fusion.44
  37.9 1.4 fusion.46
  39.4 1.5 fusion.45
  40.9 1.2 fusion.47
  42.1 0.7 pad_maximum_fusion.3
  42.8 3.4 %collective-permute-start.9 = (bf16[128,512]{0,1:T(8,128)(2,1)}, bf16[128,512]{0,1:T(8,128)(2,1)}, u32[]{:S(2)}, u32[]{:S(2)}) collective-permute-start(bf16[128,512]{0,1:T(8,128)(2,1)} %pad_maximum_fusion.3), channel_id=1, source_target_pairs={{0,1},{1,0},{2,3},{3,2},{4,5},{5,4},{6,7},{7,6},{8,9},{9,8},{10,11... | collective-permute-start | bytes 393224 | tf_op jit(solution)/shard_map/ppermute | solution.py:12
  46.2 0.9 compare_reduce_fusion.2
  47.3 18.9 %collective-permute-done = bf16[128,3584]{1,0:T(8,128)(2,1)} collective-permute-done((bf16[128,3584]{1,0:T(8,128)(2,1)}, bf16[128,3584]{1,0:T(8,128)(2,1)}, u32[]{:S(2)}, u32[]{:S(2)}) %collective-permute-start) | collective-permute-done | bytes 917536 | tf_op jit(solution)/shard_map/ppermute | solution.py:12
  66.2 2.1 %broadcast_select_fusion = (bf16[128,3584]{1,0:T(8,128)(2,1)S(1)}, bf16[128,3584]{1,0:T(8,128)(2,1)S(1)}) fusion(bf16[128,3584]{1,0:T(8,128)(2,1)} %collective-permute-done.3, pred[128]{0:T(512)(128)(4,1)S(1)} %eq.52, bf16[128,896]{1,0:T(8,128)(2,1)S(1)} %copy.100, bf16[128,896]{1,0:T(8,128)(2,1)S(1)} %copy.99, bf16[128,896]{1,0:T(8,128)(2,1)S(1)} %copy.98, ...), kind=kLoop, calls=%fused_computation.74 | loop fusion | flops 8257536 | bytes 5505152 | tf_op jit(solution)/shard_map/jit(_where)/select_n | solution.py:111
  68.3 1.9 %collective-permute-start.4 = (bf16[128,3584]{1,0:T(8,128)(2,1)S(1)}, bf16[128,3584]{1,0:T(8,128)(2,1)}, u32[]{:S(2)}, u32[]{:S(2)}) collective-permute-start(bf16[128,3584]{1,0:T(8,128)(2,1)S(1)} %get-tuple-element.37), channel_id=1, source_target_pairs={{0,8},{8,0},{16,24},{24,16},{32,40},{40,32},{48,56},{56,48},{64,72... | collective-permute-start | bytes 2752520 | tf_op jit(solution)/shard_map/ppermute | solution.py:12
  70.2 2.5 %collective-permute-start.1 = (bf16[128,3584]{1,0:T(8,128)(2,1)S(1)}, bf16[128,3584]{1,0:T(8,128)(2,1)}, u32[]{:S(2)}, u32[]{:S(2)}) collective-permute-start(bf16[128,3584]{1,0:T(8,128)(2,1)S(1)} %get-tuple-element.38), channel_id=1, source_target_pairs={{0,8},{8,0},{16,24},{24,16},{32,40},{40,32},{48,56},{56,48},{64,72... | collective-permute-start | bytes 2752520 | tf_op jit(solution)/shard_map/ppermute | solution.py:12
  72.8 1.8 fusion.40
  74.6 1.8 fusion.42
  76.4 1.8 fusion.41
  78.2 1.7 fusion.43
  80.0 3.4 %collective-permute-start.6 = (bf16[128,512]{0,1:T(8,128)(2,1)S(1)}, bf16[128,512]{0,1:T(8,128)(2,1)S(1)}, u32[]{:S(2)}, u32[]{:S(2)}) collective-permute-start(bf16[128,512]{0,1:T(8,128)(2,1)S(1)} %pad_maximum_fusion.2), channel_id=1, source_target_pairs={{0,1},{1,0},{2,3},{3,2},{4,5},{5,4},{6,7},{7,6},{8,9},{9,8},{10,11... | collective-permute-start | bytes 393224 | tf_op jit(solution)/shard_map/ppermute | solution.py:12
  83.6 2.0 %broadcast_select_fusion.2 = (bf16[128,3584]{1,0:T(8,128)(2,1)S(1)}, bf16[128,3584]{1,0:T(8,128)(2,1)S(1)}) fusion(bf16[128,3584]{1,0:T(8,128)(2,1)} %collective-permute-done.4, bf16[128,3584]{1,0:T(8,128)(2,1)S(1)} %get-tuple-element.37, pred[128]{0:T(512)(128)(4,1)S(1)} %eq.49, bf16[128,3584]{1,0:T(8,128)(2,1)} %collective-permute-done.1, ...), kind=kLoop, calls=%fused_computation.76 | loop fusion | flops 917504 | bytes 5505152 | tf_op jit(solution)/shard_map/jit(_where)/select_n | solution.py:111
  85.6 3.8 %collective-permute-start.5 = (bf16[128,3584]{1,0:T(8,128)(2,1)S(1)}, bf16[128,3584]{1,0:T(8,128)(2,1)S(1)}, u32[]{:S(2)}, u32[]{:S(2)}) collective-permute-start(bf16[128,3584]{1,0:T(8,128)(2,1)S(1)} %get-tuple-element.35), channel_id=1, source_target_pairs={{0,256},{8,264},{16,272},{24,280},{32,288},{40,296},{48,304},{56,3... | collective-permute-start | bytes 2752520 | tf_op jit(solution)/shard_map/ppermute | solution.py:12
  89.4 5.9 %collective-permute-start.2 = (bf16[128,3584]{1,0:T(8,128)(2,1)S(1)}, bf16[128,3584]{1,0:T(8,128)(2,1)}, u32[]{:S(2)}, u32[]{:S(2)}) collective-permute-start(bf16[128,3584]{1,0:T(8,128)(2,1)S(1)} %get-tuple-element.36), channel_id=1, source_target_pairs={{0,256},{8,264},{16,272},{24,280},{32,288},{40,296},{48,304},{56,3... | collective-permute-start | bytes 2752520 | tf_op jit(solution)/shard_map/ppermute | solution.py:12
  95.4 1.0 broadcast_select_fusion.6
  96.3 1.9 %collective-permute-start.10 = (bf16[128,512]{0,1:T(8,128)(2,1)S(1)}, bf16[128,512]{0,1:T(8,128)(2,1)S(1)}, u32[]{:S(2)}, u32[]{:S(2)}) collective-permute-start(bf16[128,512]{0,1:T(8,128)(2,1)S(1)} %get-tuple-element.31), channel_id=1, source_target_pairs={{0,8},{8,0},{16,24},{24,16},{32,40},{40,32},{48,56},{56,48},{64,72... | collective-permute-start | bytes 393224 | tf_op jit(solution)/shard_map/ppermute | solution.py:12
  98.3 2.4 %collective-permute-start.7 = (bf16[128,512]{0,1:T(8,128)(2,1)S(1)}, bf16[128,512]{0,1:T(8,128)(2,1)S(1)}, u32[]{:S(2)}, u32[]{:S(2)}) collective-permute-start(bf16[128,512]{0,1:T(8,128)(2,1)S(1)} %get-tuple-element.32), channel_id=1, source_target_pairs={{0,8},{8,0},{16,24},{24,16},{32,40},{40,32},{48,56},{56,48},{64,72... | collective-permute-start | bytes 393224 | tf_op jit(solution)/shard_map/ppermute | solution.py:12
  100.7 1.0 collective-permute-done.7
  101.7 3.8 %collective-permute-start.11 = (bf16[128,512]{0,1:T(8,128)(2,1)S(1)}, bf16[128,512]{0,1:T(8,128)(2,1)S(1)}, u32[]{:S(2)}, u32[]{:S(2)}) collective-permute-start(bf16[128,512]{0,1:T(8,128)(2,1)S(1)} %get-tuple-element.29), channel_id=1, source_target_pairs={{0,256},{8,264},{16,272},{24,280},{32,288},{40,296},{48,304},{56,3... | collective-permute-start | bytes 393224 | tf_op jit(solution)/shard_map/ppermute | solution.py:12
  105.5 5.9 %collective-permute-start.8 = (bf16[128,512]{0,1:T(8,128)(2,1)S(1)}, bf16[128,512]{0,1:T(8,128)(2,1)S(1)}, u32[]{:S(2)}, u32[]{:S(2)}) collective-permute-start(bf16[128,512]{0,1:T(8,128)(2,1)S(1)} %get-tuple-element.30), channel_id=1, source_target_pairs={{0,256},{8,264},{16,272},{24,280},{32,288},{40,296},{48,304},{56,3... | collective-permute-start | bytes 393224 | tf_op jit(solution)/shard_map/ppermute | solution.py:12
  111.6 70.1 %collective-permute-done.11 = bf16[128,512]{0,1:T(8,128)(2,1)S(1)} collective-permute-done((bf16[128,512]{0,1:T(8,128)(2,1)S(1)}, bf16[128,512]{0,1:T(8,128)(2,1)S(1)}, u32[]{:S(2)}, u32[]{:S(2)}) %collective-permute-start.11) | collective-permute-done | bytes 131104 | tf_op jit(solution)/shard_map/ppermute | solution.py:12
  181.7 1.5 collective-permute-done.8
  183.3 0.8 copy.110
  184.0 0.8 copy.109
  184.8 2.6 %broadcast_select_fusion.4 = (bf16[128,3584]{1,0:T(8,128)(2,1)}, bf16[128,3584]{1,0:T(8,128)(2,1)}) fusion(bf16[128,3584]{1,0:T(8,128)(2,1)S(1)} %collective-permute-done.5, bf16[128,3584]{1,0:T(8,128)(2,1)S(1)} %get-tuple-element.35, pred[128]{0:T(512)(128)(4,1)S(1)} %eq.46, bf16[128,3584]{1,0:T(8,128)(2,1)} %collective-permute-done.2, ...), kind=kLoop, calls=%fused_computation.78 | loop fusion | flops 917504 | bytes 5505152 | tf_op jit(solution)/shard_map/jit(_where)/select_n | solution.py:111
  (99 shorter events, 2.5 us)
Async XLA Ops:
  3.8 3.5 %copy-start.27 = (bf16[128,512]{1,0:T(8,128)(2,1)S(1)}, bf16[128,512]{1,0:T(8,128)(2,1)}, u32[]{:S(2)}) copy-start(bf16[128,512]{1,0:T(8,128)(2,1)} %param.8) | copy-start | bytes 393220
  4.0 6.5 %copy-start.18 = (bf16[128,896]{0,1:T(8,128)(2,1)}, bf16[128,896]{0,1:T(8,128)(2,1)S(1)}, u32[]{:S(2)}) copy-start(bf16[128,896]{0,1:T(8,128)(2,1)S(1)} %copy.152) | copy-start | bytes 688132
  4.2 24.3 %copy-start.16 = (bf16[128,896]{0,1:T(8,128)(2,1)}, bf16[128,896]{0,1:T(8,128)(2,1)S(1)}, u32[]{:S(2)}) copy-start(bf16[128,896]{0,1:T(8,128)(2,1)S(1)} %copy.156) | copy-start | bytes 688132
  4.4 22.2 %copy-start.14 = (bf16[128,896]{0,1:T(8,128)(2,1)}, bf16[128,896]{0,1:T(8,128)(2,1)S(1)}, u32[]{:S(2)}) copy-start(bf16[128,896]{0,1:T(8,128)(2,1)S(1)} %copy.154) | copy-start | bytes 688132
  4.6 20.1 %copy-start.11 = (bf16[128,896]{0,1:T(8,128)(2,1)}, bf16[128,896]{0,1:T(8,128)(2,1)S(1)}, u32[]{:S(2)}) copy-start(bf16[128,896]{0,1:T(8,128)(2,1)S(1)} %copy.158) | copy-start | bytes 688132
  8.4 16.3 %copy-start.28 = (f32[7,128]{1,0:T(8,128)}, f32[7,128]{1,0:T(8,128)S(1)}, u32[]{:S(2)}) copy-start(f32[7,128]{1,0:T(8,128)S(1)} %get-tuple-element.39) | copy-start | bytes 10756
  9.4 17.2 %copy-start.30 = (f32[7,128]{1,0:T(8,128)}, f32[7,128]{1,0:T(8,128)S(1)}, u32[]{:S(2)}) copy-start(f32[7,128]{1,0:T(8,128)S(1)} %get-tuple-element.43) | copy-start | bytes 10756
  9.4 2.1 %copy-start.2 = (bf16[128,3584]{1,0:T(8,128)(2,1)S(1)}, bf16[128,3584]{1,0:T(8,128)(2,1)}, u32[]{:S(2)}) copy-start(bf16[128,3584]{1,0:T(8,128)(2,1)} %param.10) | copy-start | bytes 2752516
  10.5 27.4 %copy-start.32 = (f32[7,128]{1,0:T(8,128)}, f32[7,128]{1,0:T(8,128)S(1)}, u32[]{:S(2)}) copy-start(f32[7,128]{1,0:T(8,128)S(1)} %get-tuple-element.41) | copy-start | bytes 10756
  11.6 24.9 %copy-start.34 = (f32[7,128]{1,0:T(8,128)}, f32[7,128]{1,0:T(8,128)S(1)}, u32[]{:S(2)}) copy-start(f32[7,128]{1,0:T(8,128)S(1)} %get-tuple-element.45) | copy-start | bytes 10756
  11.6 0.9 copy-start.23
  11.8 2.5 %copy-start.3 = (bf16[128,896]{0,1:T(8,128)(2,1)}, bf16[128,896]{0,1:T(8,128)(2,1)S(1)}, u32[]{:S(2)}) copy-start(bf16[128,896]{0,1:T(8,128)(2,1)S(1)} %copy.159) | copy-start | bytes 688132
  12.7 3.9 %copy-start.7 = (f32[7,128,128]{1,2,0:T(8,128)}, f32[7,128,128]{1,2,0:T(8,128)S(1)}, u32[]{:S(2)}) copy-start(f32[7,128,128]{1,2,0:T(8,128)S(1)} %convolution_bitcast_fusion.3) | copy-start | bytes 1376260
  14.9 1.7 copy-start.8
  17.1 1.6 copy-start.9
  19.1 1.9 copy-start.5
  19.4 1.7 copy-start.10
  21.2 3.5 %copy-start.24 = (bf16[128,512]{1,0:T(8,128)(2,1)S(1)}, bf16[128,512]{1,0:T(8,128)(2,1)}, u32[]{:S(2)}) copy-start(bf16[128,512]{1,0:T(8,128)(2,1)} %param.9) | copy-start | bytes 393220
  21.3 26.0 %collective-permute-start.3 = (bf16[128,3584]{1,0:T(8,128)(2,1)S(1)}, bf16[128,3584]{1,0:T(8,128)(2,1)}, u32[]{:S(2)}, u32[]{:S(2)}) collective-permute-start(bf16[128,3584]{1,0:T(8,128)(2,1)S(1)} %pad_maximum_fusion.1), channel_id=1, source_target_pairs={{0,1},{1,0},{2,3},{3,2},{4,5},{5,4},{6,7},{7,6},{8,9},{9,8},{10,11... | collective-permute-start | bytes 2752520 | tf_op jit(solution)/shard_map/ppermute | solution.py:12
  28.5 1.9 %copy-start.19 = (bf16[128,896]{0,1:T(8,128)(2,1)S(1)}, bf16[128,896]{0,1:T(8,128)(2,1)}, u32[]{:S(2)}) copy-start(bf16[128,896]{0,1:T(8,128)(2,1)} %copy-done.18) | copy-start | bytes 688132
  30.4 1.3 copy-start.22
  30.4 1.5 copy-start.21
  31.7 0.9 copy-start.20
  33.0 6.4 %copy-start.1 = (bf16[128,896]{1,0:T(8,128)(2,1)}, bf16[128,896]{1,0:T(8,128)(2,1)S(1)}, u32[]{:S(2)}) copy-start(bf16[128,896]{1,0:T(8,128)(2,1)S(1)} %copy.73) | copy-start | bytes 688132
  33.0 3.5 %copy-start.4 = (bf16[128,896]{0,1:T(8,128)(2,1)S(1)}, bf16[128,896]{0,1:T(8,128)(2,1)}, u32[]{:S(2)}) copy-start(bf16[128,896]{0,1:T(8,128)(2,1)} %copy-done.3) | copy-start | bytes 688132
  34.0 32.2 %collective-permute-start = (bf16[128,3584]{1,0:T(8,128)(2,1)}, bf16[128,3584]{1,0:T(8,128)(2,1)}, u32[]{:S(2)}, u32[]{:S(2)}) collective-permute-start(bf16[128,3584]{1,0:T(8,128)(2,1)} %pad_maximum_fusion), channel_id=1, source_target_pairs={{0,1},{1,0},{2,3},{3,2},{4,5},{5,4},{6,7},{7,6},{8,9},{9,8},{10,11... | collective-permute-start | bytes 2752520 | tf_op jit(solution)/shard_map/ppermute | solution.py:12
  39.4 1.5 copy-start.6
  39.4 1.5 copy-start.12
  42.1 5.2 %copy-start.25 = (bf16[128,128]{0,1:T(8,128)(2,1)}, bf16[128,128]{0,1:T(8,128)(2,1)S(1)}, u32[]{:S(2)}) copy-start(bf16[128,128]{0,1:T(8,128)(2,1)S(1)} %fusion.47) | copy-start | bytes 98308
  42.8 52.5 %collective-permute-start.9 = (bf16[128,512]{0,1:T(8,128)(2,1)}, bf16[128,512]{0,1:T(8,128)(2,1)}, u32[]{:S(2)}, u32[]{:S(2)}) collective-permute-start(bf16[128,512]{0,1:T(8,128)(2,1)} %pad_maximum_fusion.3), channel_id=1, source_target_pairs={{0,1},{1,0},{2,3},{3,2},{4,5},{5,4},{6,7},{7,6},{8,9},{9,8},{10,11... | collective-permute-start | bytes 393224 | tf_op jit(solution)/shard_map/ppermute | solution.py:12
  47.3 25.5 %copy-start.35 = (f32[7,128]{1,0:T(8,128)S(1)}, f32[7,128]{1,0:T(8,128)}, u32[]{:S(2)}) copy-start(f32[7,128]{1,0:T(8,128)} %copy-done.34) | copy-start | bytes 10756
  68.3 6.3 %copy-start = (bf16[128,3584]{1,0:T(8,128)(2,1)}, bf16[128,3584]{1,0:T(8,128)(2,1)S(1)}, u32[]{:S(2)}) copy-start(bf16[128,3584]{1,0:T(8,128)(2,1)S(1)} %get-tuple-element.38) | copy-start | bytes 2752516
  68.3 15.3 %collective-permute-start.4 = (bf16[128,3584]{1,0:T(8,128)(2,1)S(1)}, bf16[128,3584]{1,0:T(8,128)(2,1)}, u32[]{:S(2)}, u32[]{:S(2)}) collective-permute-start(bf16[128,3584]{1,0:T(8,128)(2,1)S(1)} %get-tuple-element.37), channel_id=1, source_target_pairs={{0,8},{8,0},{16,24},{24,16},{32,40},{40,32},{48,56},{56,48},{64,72... | collective-permute-start | bytes 2752520 | tf_op jit(solution)/shard_map/ppermute | solution.py:12
  70.2 4.4 %copy-start.17 = (bf16[128,896]{0,1:T(8,128)(2,1)S(1)}, bf16[128,896]{0,1:T(8,128)(2,1)}, u32[]{:S(2)}) copy-start(bf16[128,896]{0,1:T(8,128)(2,1)} %copy-done.16) | copy-start | bytes 688132
  70.2 4.4 %copy-start.33 = (f32[7,128]{1,0:T(8,128)S(1)}, f32[7,128]{1,0:T(8,128)}, u32[]{:S(2)}) copy-start(f32[7,128]{1,0:T(8,128)} %copy-done.32) | copy-start | bytes 10756
  70.2 13.4 %collective-permute-start.1 = (bf16[128,3584]{1,0:T(8,128)(2,1)S(1)}, bf16[128,3584]{1,0:T(8,128)(2,1)}, u32[]{:S(2)}, u32[]{:S(2)}) collective-permute-start(bf16[128,3584]{1,0:T(8,128)(2,1)S(1)} %get-tuple-element.38), channel_id=1, source_target_pairs={{0,8},{8,0},{16,24},{24,16},{32,40},{40,32},{48,56},{56,48},{64,72... | collective-permute-start | bytes 2752520 | tf_op jit(solution)/shard_map/ppermute | solution.py:12
  74.6 1.8 copy-start.15
  74.6 1.8 copy-start.31
  76.4 1.8 copy-start.13
  76.4 1.8 copy-start.29
  80.0 15.3 %collective-permute-start.6 = (bf16[128,512]{0,1:T(8,128)(2,1)S(1)}, bf16[128,512]{0,1:T(8,128)(2,1)S(1)}, u32[]{:S(2)}, u32[]{:S(2)}) collective-permute-start(bf16[128,512]{0,1:T(8,128)(2,1)S(1)} %pad_maximum_fusion.2), channel_id=1, source_target_pairs={{0,1},{1,0},{2,3},{3,2},{4,5},{5,4},{6,7},{7,6},{8,9},{9,8},{10,11... | collective-permute-start | bytes 393224 | tf_op jit(solution)/shard_map/ppermute | solution.py:12
  83.6 11.8 %copy-start.26 = (bf16[128,128]{0,1:T(8,128)(2,1)S(1)}, bf16[128,128]{0,1:T(8,128)(2,1)}, u32[]{:S(2)}) copy-start(bf16[128,128]{0,1:T(8,128)(2,1)} %copy-done.25) | copy-start | bytes 98308
  85.6 99.3 %collective-permute-start.5 = (bf16[128,3584]{1,0:T(8,128)(2,1)S(1)}, bf16[128,3584]{1,0:T(8,128)(2,1)S(1)}, u32[]{:S(2)}, u32[]{:S(2)}) collective-permute-start(bf16[128,3584]{1,0:T(8,128)(2,1)S(1)} %get-tuple-element.35), channel_id=1, source_target_pairs={{0,256},{8,264},{16,272},{24,280},{32,288},{40,296},{48,304},{56,3... | collective-permute-start | bytes 2752520 | tf_op jit(solution)/shard_map/ppermute | solution.py:12
  89.4 95.4 %collective-permute-start.2 = (bf16[128,3584]{1,0:T(8,128)(2,1)S(1)}, bf16[128,3584]{1,0:T(8,128)(2,1)}, u32[]{:S(2)}, u32[]{:S(2)}) collective-permute-start(bf16[128,3584]{1,0:T(8,128)(2,1)S(1)} %get-tuple-element.36), channel_id=1, source_target_pairs={{0,256},{8,264},{16,272},{24,280},{32,288},{40,296},{48,304},{56,3... | collective-permute-start | bytes 2752520 | tf_op jit(solution)/shard_map/ppermute | solution.py:12
  96.3 4.3 %collective-permute-start.10 = (bf16[128,512]{0,1:T(8,128)(2,1)S(1)}, bf16[128,512]{0,1:T(8,128)(2,1)S(1)}, u32[]{:S(2)}, u32[]{:S(2)}) collective-permute-start(bf16[128,512]{0,1:T(8,128)(2,1)S(1)} %get-tuple-element.31), channel_id=1, source_target_pairs={{0,8},{8,0},{16,24},{24,16},{32,40},{40,32},{48,56},{56,48},{64,72... | collective-permute-start | bytes 393224 | tf_op jit(solution)/shard_map/ppermute | solution.py:12
  98.3 3.4 %collective-permute-start.7 = (bf16[128,512]{0,1:T(8,128)(2,1)S(1)}, bf16[128,512]{0,1:T(8,128)(2,1)S(1)}, u32[]{:S(2)}, u32[]{:S(2)}) collective-permute-start(bf16[128,512]{0,1:T(8,128)(2,1)S(1)} %get-tuple-element.32), channel_id=1, source_target_pairs={{0,8},{8,0},{16,24},{24,16},{32,40},{40,32},{48,56},{56,48},{64,72... | collective-permute-start | bytes 393224 | tf_op jit(solution)/shard_map/ppermute | solution.py:12
  101.7 80.0 %collective-permute-start.11 = (bf16[128,512]{0,1:T(8,128)(2,1)S(1)}, bf16[128,512]{0,1:T(8,128)(2,1)S(1)}, u32[]{:S(2)}, u32[]{:S(2)}) collective-permute-start(bf16[128,512]{0,1:T(8,128)(2,1)S(1)} %get-tuple-element.29), channel_id=1, source_target_pairs={{0,256},{8,264},{16,272},{24,280},{32,288},{40,296},{48,304},{56,3... | collective-permute-start | bytes 393224 | tf_op jit(solution)/shard_map/ppermute | solution.py:12
  105.5 77.7 %collective-permute-start.8 = (bf16[128,512]{0,1:T(8,128)(2,1)S(1)}, bf16[128,512]{0,1:T(8,128)(2,1)S(1)}, u32[]{:S(2)}, u32[]{:S(2)}) collective-permute-start(bf16[128,512]{0,1:T(8,128)(2,1)S(1)} %get-tuple-element.30), channel_id=1, source_target_pairs={{0,256},{8,264},{16,272},{24,280},{32,288},{40,296},{48,304},{56,3... | collective-permute-start | bytes 393224 | tf_op jit(solution)/shard_map/ppermute | solution.py:12
where the time goes:
time: 191 us; the launch traced here: 187 us
  waiting for transfers between devices  91.5 us (48%)
  starting transfers between devices  40.9 us (21%)
  matrix products  31.2 us (16%)
  other arithmetic  13.1 us (7%)
  local copies, waits for them, and re-layouts  9.33 us (5%)
    ppermute x12, waiting for transfers between devices, partner_2(): lax.ppermute(shard, axis, [(i, i ^ 1 << bit) for i in range(lax.axis_size...  91.5 us
    ppermute x12, starting transfers between devices, partner_2(): lax.ppermute(shard, axis, [(i, i ^ 1 << bit) for i in range(lax.axis_size...  40.9 us
    select_n x6, other arithmetic, body(): jnp.where(row_flags[:, None], got, own)  7.76 us
    dot_general x4, matrix products, attend_local(): jnp.einsum('grs,rgd->sd', dscore, qh, preferred_element_type=jnp.float32)  7.08 us
    dot_general x4, matrix products, attend_local(): jnp.einsum('grs,sd->rgd', probs_b, vh, preferred_element_type=jnp.float32)  7.01 us
    dot_general x4, matrix products, attend_local(): jnp.einsum('grs,sd->rgd', dscore, kh, preferred_element_type=jnp.float32)  6.5 us
    dot_general x4, matrix products, attend_local(): jnp.einsum('grs,rgd->sd', probs_b, dh, preferred_element_type=jnp.float32)  5.51 us
    unnamed x82, local copies, waits for them, and re-layouts  4.29 us
  transfers between devices with their start and end apart: 12, of which 4 were waited for; matrix products, arithmetic and copies ran while one was open for 16% of the time, Pallas kernels for 0%

commit v1 on v0

v1 whole, which is shorter than its diff:
```python
import functools

import jax
import jax.numpy as jnp
from jax import lax
from jax.experimental import pallas as pl
from jax.experimental.pallas import tpu as pltpu
from jax.sharding import PartitionSpec as P

HD = 128
KVH = 4
GROUP = 7
BLOCK = 64
SEQ = 2 * BLOCK
SCALE = 1.0 / HD**0.5
PAIR = 2 * GROUP * HD
TRI = GROUP * BLOCK
DIAG = 16
SIDE = 2 * BLOCK
ROWS = TRI + DIAG + 4 * SIDE
AT = TRI + DIAG
VMEM_LIMIT = 48 * 1024 * 1024

NT = (((1,), (1,)), ((), ()))
NN = (((1,), (0,)), ((), ()))
TN = (((0,), (0,)), ((), ()))


def mm(a, b, dims):
    return lax.dot_general(a, b, dims, preferred_element_type=jnp.float32)


def iota(shape, dim):
    return lax.broadcasted_iota(jnp.int32, shape, dim)


def fold_matrix():
    shape = (BLOCK, 2 * BLOCK)
    return jnp.where((iota(shape, 1) & (BLOCK - 1)) == iota(shape, 0), 1.0, 0.0).astype(jnp.bfloat16)


def turn(fold, pair):
    low = iota(pair.shape, 1) < BLOCK
    zero = jnp.zeros_like(pair)
    split = jnp.concatenate([jnp.where(low, pair, zero), jnp.where(low, zero, pair)], 0)
    return mm(fold, split, NT)


def pack_kernel(chunk, head_rows, valid_ref, q_ref, k_ref, v_ref, g_ref, *refs):
    other_ref = refs[0] if head_rows else None
    pack_ref, qbd, gbd = refs[-3:]
    zero = jnp.zeros((BLOCK, HD), jnp.bfloat16)
    for full, ref in ((qbd, q_ref), (gbd, g_ref)):
        for h in range(GROUP):
            r = h * 2 * BLOCK
            full[r : r + BLOCK, 0:HD] = ref[:, h * HD : (h + 1) * HD]
            full[r : r + BLOCK, HD:] = zero
            full[r + BLOCK : r + 2 * BLOCK, 0:HD] = zero
            full[r + BLOCK : r + 2 * BLOCK, HD:] = ref[:, (GROUP + h) * HD : (GROUP + h + 1) * HD]
    wide = (BLOCK, GROUP * 2 * BLOCK)
    key_pos = iota(wide, 0)
    query_pos = iota(wide, 1) & (BLOCK - 1)
    allow = (key_pos <= query_pos) & (key_pos < valid_ref[0])
    score = jnp.where(allow, mm(k_ref[...], qbd[...], NT) * SCALE, -1e30)
    weights = jnp.exp(score - jnp.max(score, axis=0, keepdims=True))
    probs = weights / jnp.sum(weights, axis=0, keepdims=True)
    probs_b = probs.astype(jnp.bfloat16)
    dprob = mm(v_ref[...], gbd[...], NT)
    delta = jnp.sum(probs * dprob, axis=0, keepdims=True)
    dscore = (probs * (dprob - delta) * SCALE).astype(jnp.bfloat16)
    dv = mm(probs_b, gbd[...], NN).astype(jnp.bfloat16)
    dk = mm(dscore, qbd[...], NN).astype(jnp.bfloat16)

    fold = fold_matrix()
    square = (BLOCK, 2 * BLOCK)
    row, lane = iota(square, 0), iota(square, 1) & (BLOCK - 1)
    diag = []
    for h in range(GROUP):
        cut = slice(h * 2 * BLOCK, (h + 1) * 2 * BLOCK)
        ds = dscore[:, cut]
        pack_ref[h * BLOCK : (h + 1) * BLOCK, :] = jnp.where(
            row <= lane, probs_b[:, cut].astype(jnp.float32), turn(fold, ds)
        ).astype(jnp.bfloat16)
        diag.append(
            jnp.sum(jnp.where(row == lane, ds.astype(jnp.float32), 0.0), axis=0, keepdims=True)
        )
    diag.append(jnp.zeros((DIAG - GROUP, 2 * BLOCK), jnp.float32))
    pack_ref[TRI:AT, :] = jnp.concatenate(diag, 0).astype(jnp.bfloat16)
    for i, part in enumerate((k_ref[...], v_ref[...], dk, dv)):
        for j in range(2):
            r = AT + i * SIDE + j * BLOCK
            pack_ref[r : r + BLOCK, :] = part[:, j * HD : (j + 1) * HD]
    if head_rows:
        pack_ref[ROWS:, :] = other_ref[...]


def make_pack(chunk, valid, q, k, v, g, other=None):
    rows = ROWS if other is None else 2 * ROWS
    wide = pl.BlockSpec((BLOCK, PAIR), lambda i: (1, chunk))
    thin = pl.BlockSpec((BLOCK, 2 * HD), lambda i: (1, chunk))
    specs = [pl.BlockSpec(memory_space=pltpu.SMEM), wide, thin, thin, wide]
    args = [valid, q, k, v, g]
    if other is not None:
        specs.append(pl.BlockSpec((ROWS, HD), lambda i: (0, 0)))
        args.append(other)
    return pl.pallas_call(
        functools.partial(pack_kernel, chunk, other is not None),
        grid=(1,),
        out_shape=jax.ShapeDtypeStruct((rows, HD), jnp.bfloat16),
        in_specs=specs,
        out_specs=pl.BlockSpec((rows, HD), lambda i: (0, 0)),
        scratch_shapes=[pltpu.VMEM((GROUP * 2 * BLOCK, 2 * HD), jnp.bfloat16)] * 2,
        compiler_params=pltpu.CompilerParams(vmem_limit_bytes=VMEM_LIMIT),
        cost_estimate=pl.CostEstimate(
            flops=8 * BLOCK * GROUP * 2 * BLOCK * 2 * HD, bytes_accessed=1 << 20, transcendentals=0
        ),
        name="pack_rows",
    )(*args)


def own_kernel(first_ref, valid_ref, q_ref, k_ref, v_ref, g_ref, o_ref, dq_ref, dk_ref, dv_ref):
    k, v = k_ref[...], v_ref[...]
    q = jnp.concatenate([q_ref[:, h * HD : (h + 1) * HD] for h in range(GROUP)], 0)
    g = jnp.concatenate([g_ref[:, h * HD : (h + 1) * HD] for h in range(GROUP)], 0)
    wide = (SEQ, GROUP * SEQ)
    key_pos = iota(wide, 0)
    query_pos = iota(wide, 1) & (SEQ - 1)
    start = jnp.where(query_pos < BLOCK, first_ref[0], first_ref[1]) * BLOCK
    live = jnp.where(key_pos < BLOCK, valid_ref[0], valid_ref[1])
    allow = (key_pos >= start) & (key_pos <= query_pos) & ((key_pos & (BLOCK - 1)) < live)
    score = jnp.where(allow, mm(k, q, NT) * SCALE, -1e30)
    weights = jnp.exp(score - jnp.max(score, axis=0, keepdims=True))
    probs = weights / jnp.sum(weights, axis=0, keepdims=True)
    probs_b = probs.astype(jnp.bfloat16)
    dprob = mm(v, g, NT)
    delta = jnp.sum(probs * dprob, axis=0, keepdims=True)
    dscore = (probs * (dprob - delta) * SCALE).astype(jnp.bfloat16)
    dv_ref[...] = mm(probs_b, g, NN).astype(jnp.bfloat16)
    dk_ref[...] = mm(dscore, q, NN).astype(jnp.bfloat16)
    for h in range(GROUP):
        cut = slice(h * SEQ, (h + 1) * SEQ)
        o_ref[:, h * HD : (h + 1) * HD] = mm(probs_b[:, cut], v, TN).astype(jnp.bfloat16)
        dq_ref[:, h * HD : (h + 1) * HD] = mm(dscore[:, cut], k, TN).astype(jnp.bfloat16)


def own_attention(first, valid, q, k, v, g):
    wide = pl.BlockSpec((SEQ, GROUP * HD), lambda i: (0, i))
    thin = pl.BlockSpec((SEQ, HD), lambda i: (0, i))
    smem = pl.BlockSpec(memory_space=pltpu.SMEM)
    return pl.pallas_call(
        own_kernel,
        grid=(KVH,),
        out_shape=[jax.ShapeDtypeStruct(x.shape, jnp.bfloat16) for x in (q, q, k, v)],
        in_specs=[smem, smem, wide, thin, thin, wide],
        out_specs=[wide, wide, thin, thin],
        compiler_params=pltpu.CompilerParams(vmem_limit_bytes=VMEM_LIMIT),
        cost_estimate=pl.CostEstimate(
            flops=12 * KVH * GROUP * SEQ * SEQ * HD, bytes_accessed=4 << 20, transcendentals=0
        ),
        name="own_attention",
    )(first, valid, q, k, v, g)


def place_kernel(chunk, sources, pick_ref, *refs):
    packs = refs[:sources]
    o_ref, dq_ref, dk_ref, dv_ref, pack, o_buf, dq_buf, side, sem = refs[sources + 4 :]
    pick = pick_ref[0]
    for i, ref in enumerate(packs):

        @pl.when(pick == i)
        def _():
            got = pltpu.make_async_copy(ref, pack, sem.at[4])
            got.start()
            got.wait()

    @pl.when(pick < sources)
    def _():
        fold = fold_matrix()
        square = (BLOCK, 2 * BLOCK)
        row, lane = iota(square, 0), iota(square, 1) & (BLOCK - 1)
        zero = jnp.zeros((BLOCK, HD), jnp.bfloat16)

        def spread(i):
            r = AT + i * SIDE
            return jnp.concatenate(
                [
                    jnp.concatenate([pack[r : r + BLOCK, :], zero], 1),
                    jnp.concatenate([zero, pack[r + BLOCK : r + SIDE, :]], 1),
                ],
                0,
            )

        kbd, vbd = spread(0), spread(1)
        for j in range(2):
            for i in range(2):
                r = AT + (2 + i) * SIDE + j * BLOCK
                side[i, :, j * HD : (j + 1) * HD] = pack[r : r + BLOCK, :]
        diag = pack[TRI:AT, :].astype(jnp.float32)
        probs, dscore = [], []
        for h in range(GROUP):
            both = pack[h * BLOCK : (h + 1) * BLOCK, :].astype(jnp.float32)
            upper = jnp.where(row <= lane, both, 0.0).astype(jnp.bfloat16)
            probs.append(turn(fold, upper).astype(jnp.bfloat16))
            line = jnp.where(row == lane, diag[h : h + 1, :], 0.0)
            dscore.append(jnp.where(row > lane, both, line).astype(jnp.bfloat16))
        out = mm(jnp.concatenate(probs, 0), vbd, NN).astype(jnp.bfloat16)
        dq = mm(jnp.concatenate(dscore, 0), kbd, NN).astype(jnp.bfloat16)
        for buf, val in ((o_buf, out), (dq_buf, dq)):
            for h in range(GROUP):
                for j in range(2):
                    at = (j * GROUP + h) * HD
                    buf[:, at : at + HD] = val[h * BLOCK : (h + 1) * BLOCK, j * HD : (j + 1) * HD]
        rows = pl.ds(BLOCK, BLOCK)
        copies = [
            pltpu.make_async_copy(o_buf, o_ref.at[rows, pl.ds(chunk * PAIR, PAIR)], sem.at[0]),
            pltpu.make_async_copy(dq_buf, dq_ref.at[rows, pl.ds(chunk * PAIR, PAIR)], sem.at[1]),
            pltpu.make_async_copy(
                side.at[0], dk_ref.at[rows, pl.ds(chunk * 2 * HD, 2 * HD)], sem.at[2]
            ),
            pltpu.make_async_copy(
                side.at[1], dv_ref.at[rows, pl.ds(chunk * 2 * HD, 2 * HD)], sem.at[3]
            ),
        ]
        for c in copies:
            c.start()
        for c in copies:
            c.wait()


def place(chunk, pick, packs, outs):
    n = len(packs)
    return pl.pallas_call(
        functools.partial(place_kernel, chunk, n),
        out_shape=[jax.ShapeDtypeStruct(x.shape, x.dtype) for x in outs],
        in_specs=[pl.BlockSpec(memory_space=pltpu.SMEM)] + [pl.BlockSpec(memory_space=pl.ANY)] * (n + 4),
        out_specs=[pl.BlockSpec(memory_space=pl.ANY)] * 4,
        scratch_shapes=[
            pltpu.VMEM((ROWS, HD), jnp.bfloat16),
            pltpu.VMEM((BLOCK, PAIR), jnp.bfloat16),
            pltpu.VMEM((BLOCK, PAIR), jnp.bfloat16),
            pltpu.VMEM((2, BLOCK, 2 * HD), jnp.bfloat16),
            pltpu.SemaphoreType.DMA((5,)),
        ],
        input_output_aliases={1 + n + i: i for i in range(4)},
        compiler_params=pltpu.CompilerParams(vmem_limit_bytes=VMEM_LIMIT),
        cost_estimate=pl.CostEstimate(
            flops=8 * GROUP * BLOCK * 2 * BLOCK * 2 * HD, bytes_accessed=1 << 20, transcendentals=0
        ),
        name="place_rows",
    )(pick, *packs, *outs)


def swap(shard, axis, bit):
    return lax.ppermute(shard, axis, [(i, i ^ 1 << bit) for i in range(lax.axis_size(axis))])


def body(queries, keys, values, out_grad, doc_first, doc_valid, move_plan):
    near = lax.axis_size("fsdp")
    top = lax.axis_size("dp").bit_length() - 2
    micro = lax.axis_index("dp") * near + lax.axis_index("fsdp")
    across = jnp.bitwise_xor(micro, near << top)
    first, valid = doc_first[micro], doc_valid[micro]
    mine, theirs = move_plan[:, micro, 1], move_plan[:, across, 1]
    f0, f1, f2 = mine[0] == 1, mine[1] == 1, mine[2] == 1
    g0, g1 = theirs[0] == 1, theirs[1] == 1

    args = (queries, keys, values, out_grad)
    pack_b = make_pack(1, valid[1:], *args)
    far_b = swap(pack_b, "dp", top)
    pack = make_pack(0, valid[1:], *args, other=pack_b)
    outs = own_attention(first, valid, *args)
    pack = jnp.where(f0, swap(pack, "fsdp", 0), pack)
    pack = jnp.where(f1, swap(pack, "dp", 0), pack)
    pack_a, pack_b = pack[:ROWS], pack[ROWS:]
    far_a = swap(pack_a, "dp", top)
    far_b = jnp.where(g0, swap(far_b, "fsdp", 0), far_b)
    near_b = swap(far_b, "dp", 0)
    still = ~(f0 | f1 | f2)
    pick_b = jnp.where(still, 3, jnp.where(f2, jnp.where(g1, 2, 1), 0)).astype(jnp.int32)
    outs = place(1, pick_b[None], (pack_b, far_b, near_b), outs)
    pick_a = jnp.where(still, 2, jnp.where(f2, 1, 0)).astype(jnp.int32)
    return tuple(place(0, pick_a[None], (pack_a, far_a), outs))


def solution(mesh):
    rows = P(("dp", "fsdp"), None)
    return jax.shard_map(
        body,
        mesh=mesh,
        in_specs=(rows,) * 4 + (P(),) * 3,
        out_specs=(rows,) * 4,
        check_vma=False,
    )
```

time: 191 us -> 64.3 us (0.34)
  the two profiles are of different devices: /device:TPU:436 before, /device:TPU:19 now
where the time goes in v1:
time: 64.3 us; the launch traced here: 63.9 us
  starting transfers between devices  22.4 us (35%)
  waiting for transfers between devices  19.3 us (30%)
  Pallas kernels  11 us (17%)
  local copies, waits for them, and re-layouts  7.01 us (11%)
  between operations  3.98 us (6%)
    ppermute x6, starting transfers between devices, swap(): lax.ppermute(shard, axis, [(i, i ^ 1 << bit) for i in range(lax.axis_size...  22.4 us
    ppermute x6, waiting for transfers between devices, swap(): lax.ppermute(shard, axis, [(i, i ^ 1 << bit) for i in range(lax.axis_size...  19.3 us
    pallas_call x1, Pallas kernels, own_attention(): pl.pallas_call(own_kernel, grid=(KVH,), out_shape=[jax.ShapeDtypeStruct(x...  4.94 us
    unnamed x16, local copies, waits for them, and re-layouts  4.19 us
    pallas_call x2, Pallas kernels, place(): pl.pallas_call(functools.partial(place_kernel, chunk, n), out_shape=[jax....  3.12 us
    pallas_call x2, Pallas kernels, make_pack(): pl.pallas_call(functools.partial(pack_kernel, chunk, other is not None),...  2.91 us
    slice x1, local copies, waits for them, and re-layouts, body(): g0, g1 = (theirs[0] == 1, theirs[1] == 1)  1.35 us
  transfers between devices with their start and end apart: 6, of which 4 were waited for; matrix products, arithmetic and copies ran while one was open for 2% of the time, Pallas kernels for 10%

profile of v1, /device:TPU:19, one launch (start us, length us, event | category | flops | bytes accessed | tf_op | source)
XLA Modules:
  0.0 63.9 jit_solution(12074473737122731267)
XLA Ops:
  0.6 0.9 %fusion = (s32[2]{0:T(128)S(1)}, s32[1,2]{0,1:T(2,128)S(1)}, s32[2]{0:T(128)S(1)}) fusion(s32[512,2]{0,1:T(2,128)} %param.12, s32[]{:T(128)S(6)} %select_n.51, s32[512,2]{0,1:T(2,128)} %param.11), kind=kLoop, calls=%fused_computation.10 | loop fusion | bytes 44 | tf_op jit(solution)/shard_map/dynamic_slice | solution.py:262
  1.5 0.5 slice.36
  2.1 0.0 copy-start
  2.1 1.2 %copy-done = bf16[128,3584]{1,0:T(8,128)(2,1)S(1)} copy-done((bf16[128,3584]{1,0:T(8,128)(2,1)S(1)}, bf16[128,3584]{1,0:T(8,128)(2,1)}, u32[]{:S(2)}) %copy-start) | copy-done | bytes 917528
  3.3 0.0 copy-start.2
  3.3 1.2 %copy-done.2 = bf16[128,3584]{1,0:T(8,128)(2,1)S(1)} copy-done((bf16[128,3584]{1,0:T(8,128)(2,1)S(1)}, bf16[128,3584]{1,0:T(8,128)(2,1)}, u32[]{:S(2)}) %copy-start.2) | copy-done | bytes 917528
  4.4 0.0 copy-start.4
  4.4 0.9 %copy-done.4 = bf16[128,512]{1,0:T(8,128)(2,1)S(1)} copy-done((bf16[128,512]{1,0:T(8,128)(2,1)S(1)}, bf16[128,512]{1,0:T(8,128)(2,1)}, u32[]{:S(2)}) %copy-start.4) | copy-done | bytes 131096
  5.3 0.0 copy-start.6
  5.3 0.9 %copy-done.6 = bf16[128,512]{1,0:T(8,128)(2,1)S(1)} copy-done((bf16[128,512]{1,0:T(8,128)(2,1)S(1)}, bf16[128,512]{1,0:T(8,128)(2,1)}, u32[]{:S(2)}) %copy-start.6) | copy-done | bytes 131096
  6.2 1.5 %pack_rows.2.refs_0_ = bf16[976,128]{1,0:T(8,128)(2,1)S(1)} custom-call(s32[1]{0:T(128)} %bitcast.4.valid_ref, bf16[128,3584]{1,0:T(8,128)(2,1)S(1)} %copy-done, bf16[128,512]{1,0:T(8,128)(2,1)S(1)} %copy-done.4, bf16[128,512]{1,0:T(8,128)(2,1)S(1)} %copy-done.6, bf16[128,3584]{1,0:T(8,128)(2,1)S(1)} %copy-done.2), custom_call_target="tpu_custom_call" | custom-call | flops 117440512 | bytes 1048576 | tf_op jit(solution)/shard_map/pack_rows/pallas_call | solution.py:106
  7.7 1.5 %pack_rows.3 = bf16[1952,128]{1,0:T(8,128)(2,1)S(1)} custom-call(s32[1]{0:T(128)} %bitcast.4.valid_ref, bf16[128,3584]{1,0:T(8,128)(2,1)S(1)} %copy-done, bf16[128,512]{1,0:T(8,128)(2,1)S(1)} %copy-done.4, bf16[128,512]{1,0:T(8,128)(2,1)S(1)} %copy-done.6, bf16[128,3584]{1,0:T(8,128)(2,1)S(1)} %copy-done.2, bf16[976,128]{1,0:T(8,128)(2,1)S(1)} %pack_rows.2.refs_0_), custom_call_target="tpu_custom_call" | custom-call | flops 117440512 | bytes 1048576 | tf_op jit(solution)/shard_map/pack_rows/pallas_call | solution.py:106
  9.2 4.0 %collective-permute-start = (bf16[1952,128]{1,0:T(8,128)(2,1)S(1)}, bf16[1952,128]{1,0:T(8,128)(2,1)S(1)}, u32[]{:S(2)}, u32[]{:S(2)}) collective-permute-start(bf16[1952,128]{1,0:T(8,128)(2,1)S(1)} %pack_rows.3), channel_id=1, source_target_pairs={{0,1},{1,0},{2,3},{3,2},{4,5},{5,4},{6,7},{7,6},{8,9},{9,8},{10,11... | collective-permute-start | bytes 1499144 | tf_op jit(solution)/shard_map/ppermute | solution.py:254
  13.2 5.7 %collective-permute-start.3 = (bf16[976,128]{1,0:T(8,128)(2,1)S(1)}, bf16[976,128]{1,0:T(8,128)(2,1)S(1)}, u32[]{:S(2)}, u32[]{:S(2)}) collective-permute-start(bf16[976,128]{1,0:T(8,128)(2,1)S(1)} %pack_rows.2.refs_0_), channel_id=1, source_target_pairs={{0,256},{8,264},{16,272},{24,280},{32,288},{40,296},{48,304},{56,3... | collective-permute-start | bytes 749576 | tf_op jit(solution)/shard_map/ppermute | solution.py:254
  18.8 1.4 %constant_dynamic-slice_fusion.3 = (s32[1,1,1]{1,2,0:T(1,128)}, s32[1,1,1]{1,2,0:T(1,128)}, s32[1,1,1]{1,2,0:T(1,128)}, s32[1,1,1]{1,2,0:T(1,128)}, s32[1,1,1]{1,2,0:T(1,128)}) fusion(s32[3,512,2]{1,2,0:T(2,128)} %param.13, s32[]{:T(128)S(6)} %select_n.58, s32[]{:T(128)S(6)} %add.16, s32[]{:T(128)S(6)} %select_n.51, s32[]{:T(128)S(6)} %add.17), kind=kLoop, calls=%fused_computation.6 | loop fusion | bytes 56 | tf_op jit(solution)/shard_map/slice | solution.py:265
  20.8 3.4 %collective-permute-done = bf16[1952,128]{1,0:T(8,128)(2,1)S(1)} collective-permute-done((bf16[1952,128]{1,0:T(8,128)(2,1)S(1)}, bf16[1952,128]{1,0:T(8,128)(2,1)S(1)}, u32[]{:S(2)}, u32[]{:S(2)}) %collective-permute-start) | collective-permute-done | bytes 499744 | tf_op jit(solution)/shard_map/ppermute | solution.py:254
  24.3 0.1 broadcast_select_fusion
  24.3 3.1 %collective-permute-start.1 = (bf16[1952,128]{1,0:T(8,128)(2,1)S(1)}, bf16[1952,128]{1,0:T(8,128)(2,1)S(1)}, u32[]{:S(2)}, u32[]{:S(2)}) collective-permute-start(bf16[1952,128]{1,0:T(8,128)(2,1)S(1)} %broadcast_select_fusion), channel_id=1, source_target_pairs={{0,8},{8,0},{16,24},{24,16},{32,40},{40,32},{48,56},{56,48},{64,72... | collective-permute-start | bytes 1499144 | tf_op jit(solution)/shard_map/ppermute | solution.py:254
  27.5 4.8 %collective-permute-done.3 = bf16[976,128]{1,0:T(8,128)(2,1)S(1)} collective-permute-done((bf16[976,128]{1,0:T(8,128)(2,1)S(1)}, bf16[976,128]{1,0:T(8,128)(2,1)S(1)}, u32[]{:S(2)}, u32[]{:S(2)}) %collective-permute-start.3) | collective-permute-done | bytes 249888 | tf_op jit(solution)/shard_map/ppermute | solution.py:254
  32.2 1.9 %collective-permute-start.4 = (bf16[976,128]{1,0:T(8,128)(2,1)S(1)}, bf16[976,128]{1,0:T(8,128)(2,1)S(1)}, u32[]{:S(2)}, u32[]{:S(2)}) collective-permute-start(bf16[976,128]{1,0:T(8,128)(2,1)S(1)} %collective-permute-done.3), channel_id=1, source_target_pairs={{0,1},{1,0},{2,3},{3,2},{4,5},{5,4},{6,7},{7,6},{8,9},{9,8},{10,11... | collective-permute-start | bytes 749576 | tf_op jit(solution)/shard_map/ppermute | solution.py:254
  35.4 5.6 %collective-permute-done.4 = bf16[976,128]{1,0:T(8,128)(2,1)S(1)} collective-permute-done((bf16[976,128]{1,0:T(8,128)(2,1)S(1)}, bf16[976,128]{1,0:T(8,128)(2,1)S(1)}, u32[]{:S(2)}, u32[]{:S(2)}) %collective-permute-start.4) | collective-permute-done | bytes 249888 | tf_op jit(solution)/shard_map/ppermute | solution.py:254
  41.1 3.4 %collective-permute-start.5 = (bf16[976,128]{1,0:T(8,128)(2,1)S(1)}, bf16[976,128]{1,0:T(8,128)(2,1)S(1)}, u32[]{:S(2)}, u32[]{:S(2)}) collective-permute-start(bf16[976,128]{1,0:T(8,128)(2,1)S(1)} %broadcast_select_fusion.2.refs_1_), channel_id=1, source_target_pairs={{0,8},{8,0},{16,24},{24,16},{32,40},{40,32},{48,56},{56,48},{64,72... | collective-permute-start | bytes 749576 | tf_op jit(solution)/shard_map/ppermute | solution.py:254
  44.5 0.0 collective-permute-done.1
  44.5 0.0 copy-start.1
  44.5 0.0 copy-start.3
  44.6 0.1 broadcast_select_fusion.1
  44.6 0.0 copy-start.5
  44.6 0.0 copy-start.7
  44.7 4.3 %collective-permute-start.2 = (bf16[976,128]{1,0:T(8,128)(2,1)S(1)}, bf16[976,128]{1,0:T(8,128)(2,1)S(1)}, u32[]{:S(2)}, u32[]{:S(2)}) collective-permute-start(bf16[976,128]{1,0:T(8,128)(2,1)S(1)} %get-tuple-element.23.refs_0_), channel_id=1, source_target_pairs={{0,256},{8,264},{16,272},{24,280},{32,288},{40,296},{48,304},{56,3... | collective-permute-start | bytes 749576 | tf_op jit(solution)/shard_map/ppermute | solution.py:254
  50.2 0.0 copy-done.1
  50.2 0.0 copy-done.3
  50.2 0.0 copy-done.5
  50.3 0.0 copy-done.7
  50.3 4.9 %own_attention.1 = (bf16[128,3584]{1,0:T(8,128)(2,1)}, bf16[128,3584]{1,0:T(8,128)(2,1)}, bf16[128,512]{1,0:T(8,128)(2,1)}, bf16[128,512]{1,0:T(8,128)(2,1)}) custom-call(s32[2]{0:T(128)S(1)} %get-tuple-element.29.first_ref, s32[2]{0:T(128)S(1)} %get-tuple-element.20.valid_ref, bf16[128,3584]{1,0:T(8,128)(2,1)S(1)} %copy-done.1, ...), custom_call_target="tpu_custom_call" | custom-call | flops 704643072 | bytes 4194304 | tf_op jit(solution)/shard_map/own_attention/pallas_call | solution.py:150
  55.2 0.0 collective-permute-done.5.refs_2_
  55.2 1.6 %place_rows.2 = (bf16[128,3584]{1,0:T(8,128)(2,1)}, bf16[128,3584]{1,0:T(8,128)(2,1)}, bf16[128,512]{1,0:T(8,128)(2,1)}, bf16[128,512]{1,0:T(8,128)(2,1)}) custom-call(s32[1]{0:T(128)} %bitcast.6.pick_ref, bf16[976,128]{1,0:T(8,128)(2,1)S(1)} %get-tuple-element.22.refs_0_, ...), custom_call_target="tpu_custom_call", output_to_operand_aliasing={{0}: (4, {}), {1}: (5, {}), {2}: (6, {}), {3}: (7, {})} | custom-call | flops 117440512 | bytes 1048576 | tf_op jit(solution)/shard_map/place_rows/pallas_call | solution.py:232
  56.8 5.5 %collective-permute-done.2.refs_1_ = bf16[976,128]{1,0:T(8,128)(2,1)S(1)} collective-permute-done((bf16[976,128]{1,0:T(8,128)(2,1)S(1)}, bf16[976,128]{1,0:T(8,128)(2,1)S(1)}, u32[]{:S(2)}, u32[]{:S(2)}) %collective-permute-start.2) | collective-permute-done | bytes 249888 | tf_op jit(solution)/shard_map/ppermute | solution.py:254
  62.3 1.5 %place_rows.3 = (bf16[128,3584]{1,0:T(8,128)(2,1)}, bf16[128,3584]{1,0:T(8,128)(2,1)}, bf16[128,512]{1,0:T(8,128)(2,1)}, bf16[128,512]{1,0:T(8,128)(2,1)}) custom-call(s32[1]{0:T(128)} %bitcast.3.pick_ref, bf16[976,128]{1,0:T(8,128)(2,1)S(1)} %get-tuple-element.23.refs_0_, ...), custom_call_target="tpu_custom_call", output_to_operand_aliasing={{0}: (3, {}), {1}: (4, {}), {2}: (5, {}), {3}: (6, {})} | custom-call | flops 117440512 | bytes 1048576 | tf_op jit(solution)/shard_map/place_rows/pallas_call | solution.py:232
  (2 shorter events, 0.1 us)
Async XLA Ops:
  2.1 1.2 %copy-start = (bf16[128,3584]{1,0:T(8,128)(2,1)S(1)}, bf16[128,3584]{1,0:T(8,128)(2,1)}, u32[]{:S(2)}) copy-start(bf16[128,3584]{1,0:T(8,128)(2,1)} %q_ref.5) | copy-start | bytes 2752516
  3.3 1.2 %copy-start.2 = (bf16[128,3584]{1,0:T(8,128)(2,1)S(1)}, bf16[128,3584]{1,0:T(8,128)(2,1)}, u32[]{:S(2)}) copy-start(bf16[128,3584]{1,0:T(8,128)(2,1)} %g_ref.5) | copy-start | bytes 2752516
  4.4 0.9 %copy-start.4 = (bf16[128,512]{1,0:T(8,128)(2,1)S(1)}, bf16[128,512]{1,0:T(8,128)(2,1)}, u32[]{:S(2)}) copy-start(bf16[128,512]{1,0:T(8,128)(2,1)} %k_ref.5) | copy-start | bytes 393220
  5.3 0.9 %copy-start.6 = (bf16[128,512]{1,0:T(8,128)(2,1)S(1)}, bf16[128,512]{1,0:T(8,128)(2,1)}, u32[]{:S(2)}) copy-start(bf16[128,512]{1,0:T(8,128)(2,1)} %v_ref.5) | copy-start | bytes 393220
  9.2 15.1 %collective-permute-start = (bf16[1952,128]{1,0:T(8,128)(2,1)S(1)}, bf16[1952,128]{1,0:T(8,128)(2,1)S(1)}, u32[]{:S(2)}, u32[]{:S(2)}) collective-permute-start(bf16[1952,128]{1,0:T(8,128)(2,1)S(1)} %pack_rows.3), channel_id=1, source_target_pairs={{0,1},{1,0},{2,3},{3,2},{4,5},{5,4},{6,7},{7,6},{8,9},{9,8},{10,11... | collective-permute-start | bytes 1499144 | tf_op jit(solution)/shard_map/ppermute | solution.py:254
  13.2 19.1 %collective-permute-start.3 = (bf16[976,128]{1,0:T(8,128)(2,1)S(1)}, bf16[976,128]{1,0:T(8,128)(2,1)S(1)}, u32[]{:S(2)}, u32[]{:S(2)}) collective-permute-start(bf16[976,128]{1,0:T(8,128)(2,1)S(1)} %pack_rows.2.refs_0_), channel_id=1, source_target_pairs={{0,256},{8,264},{16,272},{24,280},{32,288},{40,296},{48,304},{56,3... | collective-permute-start | bytes 749576 | tf_op jit(solution)/shard_map/ppermute | solution.py:254
  24.3 20.2 %collective-permute-start.1 = (bf16[1952,128]{1,0:T(8,128)(2,1)S(1)}, bf16[1952,128]{1,0:T(8,128)(2,1)S(1)}, u32[]{:S(2)}, u32[]{:S(2)}) collective-permute-start(bf16[1952,128]{1,0:T(8,128)(2,1)S(1)} %broadcast_select_fusion), channel_id=1, source_target_pairs={{0,8},{8,0},{16,24},{24,16},{32,40},{40,32},{48,56},{56,48},{64,72... | collective-permute-start | bytes 1499144 | tf_op jit(solution)/shard_map/ppermute | solution.py:254
  32.2 8.8 %collective-permute-start.4 = (bf16[976,128]{1,0:T(8,128)(2,1)S(1)}, bf16[976,128]{1,0:T(8,128)(2,1)S(1)}, u32[]{:S(2)}, u32[]{:S(2)}) collective-permute-start(bf16[976,128]{1,0:T(8,128)(2,1)S(1)} %collective-permute-done.3), channel_id=1, source_target_pairs={{0,1},{1,0},{2,3},{3,2},{4,5},{5,4},{6,7},{7,6},{8,9},{9,8},{10,11... | collective-permute-start | bytes 749576 | tf_op jit(solution)/shard_map/ppermute | solution.py:254
  41.1 14.1 %collective-permute-start.5 = (bf16[976,128]{1,0:T(8,128)(2,1)S(1)}, bf16[976,128]{1,0:T(8,128)(2,1)S(1)}, u32[]{:S(2)}, u32[]{:S(2)}) collective-permute-start(bf16[976,128]{1,0:T(8,128)(2,1)S(1)} %broadcast_select_fusion.2.refs_1_), channel_id=1, source_target_pairs={{0,8},{8,0},{16,24},{24,16},{32,40},{40,32},{48,56},{56,48},{64,72... | collective-permute-start | bytes 749576 | tf_op jit(solution)/shard_map/ppermute | solution.py:254
  44.5 5.7 %copy-start.1 = (bf16[128,3584]{1,0:T(8,128)(2,1)S(1)}, bf16[128,3584]{1,0:T(8,128)(2,1)}, u32[]{:S(2)}) copy-start(bf16[128,3584]{1,0:T(8,128)(2,1)} %q_ref.5) | copy-start | bytes 2752516
  44.5 5.7 %copy-start.3 = (bf16[128,3584]{1,0:T(8,128)(2,1)S(1)}, bf16[128,3584]{1,0:T(8,128)(2,1)}, u32[]{:S(2)}) copy-start(bf16[128,3584]{1,0:T(8,128)(2,1)} %g_ref.5) | copy-start | bytes 2752516
  44.6 5.6 %copy-start.5 = (bf16[128,512]{1,0:T(8,128)(2,1)S(1)}, bf16[128,512]{1,0:T(8,128)(2,1)}, u32[]{:S(2)}) copy-start(bf16[128,512]{1,0:T(8,128)(2,1)} %k_ref.5) | copy-start | bytes 393220
  44.6 5.6 %copy-start.7 = (bf16[128,512]{1,0:T(8,128)(2,1)S(1)}, bf16[128,512]{1,0:T(8,128)(2,1)}, u32[]{:S(2)}) copy-start(bf16[128,512]{1,0:T(8,128)(2,1)} %v_ref.5) | copy-start | bytes 393220
  44.7 17.6 %collective-permute-start.2 = (bf16[976,128]{1,0:T(8,128)(2,1)S(1)}, bf16[976,128]{1,0:T(8,128)(2,1)S(1)}, u32[]{:S(2)}, u32[]{:S(2)}) collective-permute-start(bf16[976,128]{1,0:T(8,128)(2,1)S(1)} %get-tuple-element.23.refs_0_), channel_id=1, source_target_pairs={{0,256},{8,264},{16,272},{24,280},{32,288},{40,296},{48,304},{56,3... | collective-permute-start | bytes 749576 | tf_op jit(solution)/shard_map/ppermute | solution.py:254

commit v2 on v0

v2 whole, which is shorter than its diff:
```python
import functools

import jax
import jax.numpy as jnp
from jax import lax
from jax.experimental import pallas as pl
from jax.experimental.pallas import tpu as pltpu
from jax.sharding import PartitionSpec as P

HD = 128
KVH = 4
GROUP = 7
BLOCK = 64
SEQ = 2 * BLOCK
SCALE = 1.0 / HD**0.5
PAIR = 2 * GROUP * HD
TRI = GROUP * BLOCK
DIAG = 16
SIDE = 2 * BLOCK
ROWS = TRI + DIAG + 4 * SIDE
AT = TRI + DIAG
VMEM_LIMIT = 40 * 1024 * 1024
PACK_LIMIT = 48 * 1024 * 1024

NT = (((1,), (1,)), ((), ()))
NN = (((1,), (0,)), ((), ()))
TN = (((0,), (0,)), ((), ()))


def mm(a, b, dims):
    return lax.dot_general(a, b, dims, preferred_element_type=jnp.float32)


def iota(shape, dim):
    return lax.broadcasted_iota(jnp.int32, shape, dim)


def fold_matrix():
    shape = (BLOCK, 2 * BLOCK)
    return jnp.where((iota(shape, 1) & (BLOCK - 1)) == iota(shape, 0), 1.0, 0.0).astype(jnp.bfloat16)


def turn(fold, pair):
    low = iota(pair.shape, 1) < BLOCK
    zero = jnp.zeros_like(pair)
    split = jnp.concatenate([jnp.where(low, pair, zero), jnp.where(low, zero, pair)], 0)
    return mm(fold, split, NT)


def read_moves(plan_ref, near, core, far):
    me = lax.axis_index("dp") * core + lax.axis_index("fsdp")
    base = me & ~(near + far)
    z, c = [], []
    for q in range(4):
        at = base + (q & 1) * near + (q >> 1) * far
        c.append(plan_ref[1, 1, at])
        z.append(plan_ref[0, 1, at ^ (c[q] * core)])
    y = [plan_ref[2, 1, base], plan_ref[2, 1, base + near]]
    here = ((me // near) & 1) + 2 * ((me // far) & 1)

    def pick(values, index):
        out = values[0]
        for i in range(1, len(values)):
            out = jnp.where(index == i, values[i], out)
        return out

    def origin(chip):
        crossed = pick(y, chip & 1)
        passed = chip ^ (2 * crossed)
        return pick(z, passed) ^ (2 * crossed), pick(c, passed)

    branch = y[0] + 2 * y[1] + 4 * z[0] + 8 * z[1] + 16 * z[2] + 32 * z[3]
    send = [origin(here ^ step)[1] for step in range(1, 4)]
    mine, other = origin(here)
    take = jnp.where(mine == 0, other, mine + 1)
    return branch, send, take


def fill_zeros(full):
    zero = jnp.zeros((BLOCK, HD), jnp.bfloat16)
    for h in range(GROUP):
        r = h * 2 * BLOCK
        full[r : r + BLOCK, HD:] = zero
        full[r + BLOCK : r + 2 * BLOCK, 0:HD] = zero


def fill_pair(full, rows):
    for h in range(GROUP):
        r = h * 2 * BLOCK
        full[r : r + BLOCK, 0:HD] = rows[:, h * HD : (h + 1) * HD]
        full[r + BLOCK : r + 2 * BLOCK, HD:] = rows[:, (GROUP + h) * HD : (GROUP + h + 1) * HD]


def attend(q, k, v, g, allow):
    score = jnp.where(allow, mm(k, q, NT) * SCALE, -1e30)
    weights = jnp.exp(score - jnp.max(score, axis=0, keepdims=True))
    probs = weights / jnp.sum(weights, axis=0, keepdims=True)
    probs_b = probs.astype(jnp.bfloat16)
    dprob = mm(v, g, NT)
    delta = jnp.sum(probs * dprob, axis=0, keepdims=True)
    dscore = (probs * (dprob - delta) * SCALE).astype(jnp.bfloat16)
    dv = mm(probs_b, g, NN).astype(jnp.bfloat16)
    dk = mm(dscore, q, NN).astype(jnp.bfloat16)
    return probs_b, dscore, dk, dv


def block_mask(live):
    wide = (BLOCK, GROUP * 2 * BLOCK)
    key_pos = iota(wide, 0)
    query_pos = iota(wide, 1) & (BLOCK - 1)
    return (key_pos <= query_pos) & (key_pos < live)


def pack_kernel(bits, first_hbm, valid_hbm, plan_hbm, q_hbm, k_hbm, v_hbm, g_hbm, *refs):
    pack_ref, branch_ref, send_ref, facts_ref = refs[:4]
    bufs = refs[4:8]
    first_ref, valid_ref, plan_ref, qbd, gbd, sem = refs[8:]
    q_buf, k_buf, v_buf, g_buf = bufs
    words = [
        pltpu.make_async_copy(hbm, ref, sem.at[4, i])
        for i, (hbm, ref) in enumerate(
            ((plan_hbm, plan_ref), (valid_hbm, valid_ref), (first_hbm, first_ref))
        )
    ]
    copies = []
    for block, chunk in ((1, 0), (1, 1), (0, 0), (0, 1)):
        rows = pl.ds(block * BLOCK, BLOCK)
        for i, (hbm, buf) in enumerate(zip((q_hbm, k_hbm, v_hbm, g_hbm), bufs)):
            width = buf.shape[1] // 2
            at = (rows, pl.ds(chunk * width, width))
            copies.append(pltpu.make_async_copy(hbm.at[at], buf.at[at], sem.at[len(copies) // 4, i]))
    for c in words + copies:
        c.start()
    fill_zeros(qbd)
    fill_zeros(gbd)
    for c in words:
        c.wait()
    branch, send, take = read_moves(plan_ref, *bits)
    me = lax.axis_index("dp") * bits[1] + lax.axis_index("fsdp")
    branch_ref[0] = branch
    for i in range(3):
        send_ref[i] = jnp.full((1, HD), send[i], jnp.int32)
    facts = (take, jnp.where(first_ref[1, me] == 0, 1, 0), valid_ref[0, me], valid_ref[1, me])
    for i, fact in enumerate(facts):
        facts_ref[i] = jnp.full((1, HD), fact, jnp.int32)
    allow = block_mask(valid_ref[1, me])
    fold = fold_matrix()
    square = (BLOCK, 2 * BLOCK)
    row, lane = iota(square, 0), iota(square, 1) & (BLOCK - 1)
    for chunk in range(2):
        for c in copies[4 * chunk : 4 * chunk + 4]:
            c.wait()
        base = chunk * ROWS
        heads = slice(chunk * PAIR, (chunk + 1) * PAIR)
        pair = slice(chunk * 2 * HD, (chunk + 1) * 2 * HD)
        fill_pair(qbd, q_buf.at[BLOCK:, heads])
        fill_pair(gbd, g_buf.at[BLOCK:, heads])
        k, v = k_buf[BLOCK:, pair], v_buf[BLOCK:, pair]
        probs_b, dscore, dk, dv = attend(qbd[...], k, v, gbd[...], allow)
        diag = []
        for h in range(GROUP):
            cut = slice(h * 2 * BLOCK, (h + 1) * 2 * BLOCK)
            ds = dscore[:, cut]
            pack_ref[base + h * BLOCK : base + (h + 1) * BLOCK, :] = jnp.where(
                row <= lane, probs_b[:, cut].astype(jnp.float32), turn(fold, ds)
            ).astype(jnp.bfloat16)
            diag.append(
                jnp.sum(jnp.where(row == lane, ds.astype(jnp.float32), 0.0), axis=0, keepdims=True)
            )
        diag.append(jnp.zeros((DIAG - GROUP, 2 * BLOCK), jnp.float32))
        pack_ref[base + TRI : base + AT, :] = jnp.concatenate(diag, 0).astype(jnp.bfloat16)
        for i, part in enumerate((k, v, dk, dv)):
            for j in range(2):
                r = base + AT + i * SIDE + j * BLOCK
                pack_ref[r : r + BLOCK, :] = part[:, j * HD : (j + 1) * HD]
    for c in copies[8:]:
        c.wait()


def make_pack(bits, first, valid, plan, q, k, v, g):
    hbm = pl.BlockSpec(memory_space=pltpu.HBM)
    vmem = pl.BlockSpec(memory_space=pltpu.VMEM)
    return pl.pallas_call(
        functools.partial(pack_kernel, bits),
        out_shape=[
            pltpu.VMEM((2 * ROWS, HD), jnp.bfloat16),
            jax.ShapeDtypeStruct((1,), jnp.int32),
            jax.ShapeDtypeStruct((3, 1, HD), jnp.int32),
            jax.ShapeDtypeStruct((4, 1, HD), jnp.int32),
        ]
        + [pltpu.VMEM(x.shape, x.dtype) for x in (q, k, v, g)],
        in_specs=[hbm] * 7,
        out_specs=[vmem, pl.BlockSpec(memory_space=pltpu.SMEM)] + [vmem] * 6,
        scratch_shapes=[
            pltpu.SMEM(first.shape, jnp.int32),
            pltpu.SMEM(valid.shape, jnp.int32),
            pltpu.SMEM(plan.shape, jnp.int32),
            pltpu.VMEM((GROUP * 2 * BLOCK, 2 * HD), jnp.bfloat16),
            pltpu.VMEM((GROUP * 2 * BLOCK, 2 * HD), jnp.bfloat16),
            pltpu.SemaphoreType.DMA((5, 4)),
        ],
        compiler_params=pltpu.CompilerParams(vmem_limit_bytes=PACK_LIMIT),
        cost_estimate=pl.CostEstimate(
            flops=16 * BLOCK * GROUP * 2 * BLOCK * 2 * HD, bytes_accessed=3 << 20, transcendentals=0
        ),
        name="pack_rows",
    )(*(pltpu.with_memory_space_constraint(x, pltpu.HBM) for x in (first, valid, plan, q, k, v, g)))


def own_kernel(facts_ref, q_buf, k_buf, v_buf, g_buf, *refs):
    outs, news, (qbd, gbd, sem) = refs[:4], refs[4:8], refs[8:]
    o_buf, dq_buf, dk_buf, dv_buf = news

    def write(block, part, parts):
        copies = []
        for i, (buf, out) in enumerate(zip(news, outs)):
            width = buf.shape[1] // parts
            at = (pl.ds(block * BLOCK, BLOCK), pl.ds(part * width, width))
            copies.append(pltpu.make_async_copy(buf.at[at], out.at[at], sem.at[2 * block + part, i]))
            copies[-1].start()
        return copies

    joined = jnp.max(facts_ref[1]) == 1
    live = jnp.max(facts_ref[2])

    @pl.when(jnp.logical_not(joined))
    def _():
        fill_zeros(qbd)
        fill_zeros(gbd)
        allow = block_mask(live)
        copies = []
        for chunk in range(2):
            heads = slice(chunk * PAIR, (chunk + 1) * PAIR)
            pair = slice(chunk * 2 * HD, (chunk + 1) * 2 * HD)
            fill_pair(qbd, q_buf.at[0:BLOCK, heads])
            fill_pair(gbd, g_buf.at[0:BLOCK, heads])
            k, v = k_buf[0:BLOCK, pair], v_buf[0:BLOCK, pair]
            probs_b, dscore, dk, dv = attend(qbd[...], k, v, gbd[...], allow)
            dk_buf[0:BLOCK, pair] = dk
            dv_buf[0:BLOCK, pair] = dv
            for buf, squares, other in ((o_buf, probs_b, v), (dq_buf, dscore, k)):
                val = mm(squares, other, TN).astype(jnp.bfloat16)
                for h in range(GROUP):
                    for j in range(2):
                        r, at = (2 * h + j) * BLOCK, chunk * PAIR + (j * GROUP + h) * HD
                        buf[0:BLOCK, at : at + HD] = val[r : r + BLOCK, j * HD : (j + 1) * HD]
            copies += write(0, chunk, 2)
        for c in copies:
            c.wait()

    @pl.when(joined)
    def _():
        wide = (SEQ, GROUP * SEQ)
        key_pos = iota(wide, 0)
        query_pos = iota(wide, 1) & (SEQ - 1)
        live_of = jnp.where(key_pos < BLOCK, live, jnp.max(facts_ref[3]))
        allow = (key_pos <= query_pos) & ((key_pos & (BLOCK - 1)) < live_of)

        @pl.loop(0, KVH)
        def _(i):
            one = pl.ds(pl.multiple_of(i * HD, HD), HD)

            def head(h):
                return pl.ds(pl.multiple_of((i * GROUP + h) * HD, HD), HD)

            k, v = k_buf[:, one], v_buf[:, one]
            q = jnp.concatenate([q_buf[:, head(h)] for h in range(GROUP)], 0)
            g = jnp.concatenate([g_buf[:, head(h)] for h in range(GROUP)], 0)
            probs_b, dscore, dk, dv = attend(q, k, v, g, allow)
            dk_buf[:, one] = dk
            dv_buf[:, one] = dv
            for h in range(GROUP):
                cut = slice(h * SEQ, (h + 1) * SEQ)
                o_buf[:, head(h)] = mm(probs_b[:, cut], v, TN).astype(jnp.bfloat16)
                dq_buf[:, head(h)] = mm(dscore[:, cut], k, TN).astype(jnp.bfloat16)

        for c in write(0, 0, 1) + write(1, 0, 1):
            c.wait()


def own_attention(facts, q, k, v, g):
    vmem = pl.BlockSpec(memory_space=pltpu.VMEM)
    return pl.pallas_call(
        own_kernel,
        out_shape=[jax.ShapeDtypeStruct(x.shape, jnp.bfloat16) for x in (q, q, k, v)],
        in_specs=[vmem] * 5,
        out_specs=[pl.BlockSpec(memory_space=pltpu.HBM)] * 4,
        scratch_shapes=[pltpu.VMEM(x.shape, jnp.bfloat16) for x in (q, q, k, v)]
        + [pltpu.VMEM((GROUP * 2 * BLOCK, 2 * HD), jnp.bfloat16)] * 2
        + [pltpu.SemaphoreType.DMA((4, 4))],
        compiler_params=pltpu.CompilerParams(vmem_limit_bytes=VMEM_LIMIT),
        cost_estimate=pl.CostEstimate(
            flops=12 * KVH * GROUP * SEQ * SEQ * HD, bytes_accessed=4 << 20, transcendentals=0
        ),
        name="own_attention",
    )(facts, q, k, v, g)


def place_kernel(facts_ref, pack, _o, _dq, _dk, _dv, o_ref, dq_ref, dk_ref, dv_ref, o_buf, dq_buf, side, sem):
    @pl.when(jnp.max(facts_ref[1]) == 0)
    def _():
        fold = fold_matrix()
        square = (BLOCK, 2 * BLOCK)
        row, lane = iota(square, 0), iota(square, 1) & (BLOCK - 1)
        zero = jnp.zeros((BLOCK, HD), jnp.bfloat16)
        rows = pl.ds(BLOCK, BLOCK)
        copies = []
        for chunk in range(2):
            base = chunk * ROWS

            def spread(i):
                r = base + AT + i * SIDE
                return jnp.concatenate(
                    [
                        jnp.concatenate([pack[r : r + BLOCK, :], zero], 1),
                        jnp.concatenate([zero, pack[r + BLOCK : r + SIDE, :]], 1),
                    ],
                    0,
                )

            kbd, vbd = spread(0), spread(1)
            for j in range(2):
                for i in range(2):
                    r = base + AT + (2 + i) * SIDE + j * BLOCK
                    side[chunk, i, :, j * HD : (j + 1) * HD] = pack[r : r + BLOCK, :]
            diag = pack[base + TRI : base + AT, :].astype(jnp.float32)
            probs, dscore = [], []
            for h in range(GROUP):
                both = pack[base + h * BLOCK : base + (h + 1) * BLOCK, :].astype(jnp.float32)
                upper = jnp.where(row <= lane, both, 0.0).astype(jnp.bfloat16)
                probs.append(turn(fold, upper).astype(jnp.bfloat16))
                line = jnp.where(row == lane, diag[h : h + 1, :], 0.0)
                dscore.append(jnp.where(row > lane, both, line).astype(jnp.bfloat16))
            out = mm(jnp.concatenate(probs, 0), vbd, NN).astype(jnp.bfloat16)
            dq = mm(jnp.concatenate(dscore, 0), kbd, NN).astype(jnp.bfloat16)
            for buf, val in ((o_buf, out), (dq_buf, dq)):
                for h in range(GROUP):
                    for j in range(2):
                        at = (j * GROUP + h) * HD
                        buf[chunk, :, at : at + HD] = val[
                            h * BLOCK : (h + 1) * BLOCK, j * HD : (j + 1) * HD
                        ]
            heads, pair = pl.ds(chunk * PAIR, PAIR), pl.ds(chunk * 2 * HD, 2 * HD)
            for i, (buf, to) in enumerate(
                (
                    (o_buf.at[chunk], o_ref.at[rows, heads]),
                    (dq_buf.at[chunk], dq_ref.at[rows, heads]),
                    (side.at[chunk, 0], dk_ref.at[rows, pair]),
                    (side.at[chunk, 1], dv_ref.at[rows, pair]),
                )
            ):
                copies.append(pltpu.make_async_copy(buf, to, sem.at[chunk, i]))
                copies[-1].start()
        for c in copies:
            c.wait()


def place(facts, pack, outs):
    hbm = pl.BlockSpec(memory_space=pltpu.HBM)
    return pl.pallas_call(
        place_kernel,
        out_shape=[jax.ShapeDtypeStruct(x.shape, x.dtype) for x in outs],
        in_specs=[
            pl.BlockSpec(memory_space=pltpu.VMEM),
            pl.BlockSpec(memory_space=pltpu.VMEM),
            hbm,
            hbm,
            hbm,
            hbm,
        ],
        out_specs=[hbm] * 4,
        scratch_shapes=[
            pltpu.VMEM((2, BLOCK, PAIR), jnp.bfloat16),
            pltpu.VMEM((2, BLOCK, PAIR), jnp.bfloat16),
            pltpu.VMEM((2, 2, BLOCK, 2 * HD), jnp.bfloat16),
            pltpu.SemaphoreType.DMA((2, 4)),
        ],
        input_output_aliases={2 + i: i for i in range(4)},
        compiler_params=pltpu.CompilerParams(vmem_limit_bytes=VMEM_LIMIT),
        cost_estimate=pl.CostEstimate(
            flops=16 * GROUP * BLOCK * 2 * BLOCK * 2 * HD, bytes_accessed=2 << 20, transcendentals=0
        ),
        name="place_rows",
    )(facts, pack, *outs)


def origins(branch):
    found = []
    for chip in range(4):
        crossed = branch >> (chip & 1) & 1
        passed = chip ^ 2 * crossed
        found.append(2 * crossed ^ (branch >> 2 + passed & 1))
    return found


def body(queries, keys, values, out_grad, doc_first, doc_valid, move_plan):
    core, dp = lax.axis_size("fsdp"), lax.axis_size("dp")
    near, far = 1, core * dp // 2
    bits = (near, core, far)
    args = (queries, keys, values, out_grad)
    first, valid, plan = doc_first.T, doc_valid.T, jnp.swapaxes(move_plan, 1, 2)
    pack, branch, send, facts, *held = make_pack(bits, first, valid, plan, *args)
    other = lax.ppermute(pack, "dp", [(i, i ^ 1) for i in range(dp)])
    own = own_attention(facts, *held)

    def route(index):
        found = origins(index)

        def run(pack, other, send, facts):
            take = facts[0]
            got = []
            for step in (2, 3, 1):
                if step not in found:
                    continue
                pairs = []
                for i in range(core * dp):
                    chip = i // near % 2 + 2 * (i // far % 2)
                    if found[chip] == step:
                        pairs.append((i ^ (step & 1) * near ^ (step >> 1) * far, i))
                if step == 1:
                    pairs = sorted(set(pairs) | {(b, a) for a, b in pairs})
                sent = jnp.where(send[step - 1] == 1, other, pack)
                got.append((step, lax.ppermute(sent, ("dp", "fsdp"), pairs)))
            result = jnp.where(take == 1, other, pack)
            for step, rows in got:
                result = jnp.where(take == step + 1, rows, result)
            return result

        return run

    rows = lax.switch(branch[0], [route(i) for i in range(64)], pack, other, send, facts)
    return tuple(place(facts, rows, own))


def solution(mesh):
    rows = P(("dp", "fsdp"), None)
    return jax.shard_map(
        body,
        mesh=mesh,
        in_specs=(rows,) * 4 + (P(),) * 3,
        out_specs=(rows,) * 4,
        check_vma=False,
    )
```

time: 191 us -> 38 us (0.20)
  the two profiles are of different devices: /device:TPU:436 before, /device:TPU:432 now
where the time goes in v2:
time: 38 us; the launch traced here: 37.7 us
  waiting for transfers between devices  23.9 us (63%)
  Pallas kernels  7.67 us (20%)
  starting transfers between devices  3.91 us (10%)
  between operations  1.5 us (4%)
  loops' own time  0.52 us (1%)
    ppermute x2, waiting for transfers between devices, run(): got.append((step, lax.ppermute(sent, ('dp', 'fsdp'), pairs)))  23.9 us
    pallas_call x1, Pallas kernels, make_pack(): pl.pallas_call(functools.partial(pack_kernel, bits), out_shape=[pltpu.VME...  3.21 us
    pallas_call x1, Pallas kernels, own_attention(): pl.pallas_call(own_kernel, out_shape=[jax.ShapeDtypeStruct(x.shape, jnp.b...  2.73 us
    ppermute x2, starting transfers between devices, run(): got.append((step, lax.ppermute(sent, ('dp', 'fsdp'), pairs)))  1.98 us
    ppermute x1, starting transfers between devices, body(): other = lax.ppermute(pack, 'dp', [(i, i ^ 1) for i in range(dp)])  1.92 us
    pallas_call x1, Pallas kernels, place(): pl.pallas_call(place_kernel, out_shape=[jax.ShapeDtypeStruct(x.shape, x.d...  1.73 us
  transfers between devices with their start and end apart: 3, of which 1 were waited for; matrix products, arithmetic and copies ran while one was open for 0% of the time, Pallas kernels for 7%

profile of v2, /device:TPU:432, one launch (start us, length us, event | category | flops | bytes accessed | tf_op | source)
XLA Modules:
  0.0 37.7 jit_solution(2284668134967453797)
XLA Ops:
  0.6 3.2 %pack_rows.1 = (bf16[1952,128]{1,0:T(8,128)(2,1)S(1)}, s32[1]{0:T(128)}, s32[3,1,128]{2,1,0:T(1,128)S(1)}, s32[4,1,128]{2,1,0:T(1,128)S(1)}, bf16[128,3584]{1,0:...) custom-call(s32[2,512]{1,0:T(2,128)} %bitcast.601, ...), custom_call_target="tpu_custom_call" | custom-call | flops 234881024 | bytes 3145728 | tf_op jit(solution)/shard_map/pack_rows/pallas_call | solution.py:183
  3.9 1.9 %collective-permute-start.117 = (bf16[1952,128]{1,0:T(8,128)(2,1)S(1)}, bf16[1952,128]{1,0:T(8,128)(2,1)S(1)}, u32[]{:S(2)}, u32[]{:S(2)}) collective-permute-start(bf16[1952,128]{1,0:T(8,128)(2,1)S(1)} %get-tuple-element.848), channel_id=1, source_target_pairs={{0,8},{8,0},{16,24},{24,16},{32,40},{40,32},{48,56},{56,48},{64,72... | collective-permute-start | bytes 1499144 | tf_op jit(solution)/shard_map/ppermute | solution.py:403
  6.4 2.7 %own_attention.1 = (bf16[128,3584]{1,0:T(8,128)(2,1)}, bf16[128,3584]{1,0:T(8,128)(2,1)}, bf16[128,512]{1,0:T(8,128)(2,1)}, bf16[128,512]{1,0:T(8,128)(2,1)}) custom-call(s32[4,1,128]{2,1,0:T(1,128)S(1)} %get-tuple-element.846.facts_ref, bf16[128,3584]{1,0:T(8,128)(2,1)S(1)} %get-tuple-element.850.q_buf, bf16[128,512]{1,0:T(8,128)(2,1)S(1)} %get-tuple-element.851.k_buf, ...), custom_call_target="tpu_custom_call" | custom-call | flops 704643072 | bytes 4194304 | tf_op jit(solution)/shard_map/own_attention/pallas_call | solution.py:283
  9.2 0.0 collective-permute-done.117
  9.2 26.6 %conditional.1 = (bf16[1952,128]{1,0:T(8,128)(2,1)S(1)}) conditional(s32[]{:T(128)} %bitcast.301, (s32[4,1,128]{2,1,0:T(1,128)S(1)}, bf16[1952,128]{1,0:T(8,128)(2,1)S(1)}, bf16[1952,128]{1,0:T(8,128)(2,1)S(1)}) %tuple.199, (s32[4,1,128]{2,1,0:T(1,128)S(1)}, s32[3,1,128]{2,1,0:T(1,128)S(1)}, ...), branch_computations={%region_0.1_spmd, %region_1.2_spmd, %region_2.3_spmd, %region_3.4_... | conditional | flops 1749888 | bytes 11497344 | solution.py:431
  9.4 0.1 broadcast_select_fusion.50
  9.5 0.7 %collective-permute-start.49 = (bf16[1952,128]{1,0:T(8,128)(2,1)S(1)}, bf16[1952,128]{1,0:T(8,128)(2,1)S(1)}, u32[]{:S(2)}, u32[]{:S(2)}) collective-permute-start(bf16[1952,128]{1,0:T(8,128)(2,1)S(1)} %get-tuple-element.1012), channel_id=1, source_target_pairs={{0,1},{1,0},{2,3},{3,2},{4,5},{5,4},{6,7},{7,6},{8,9},{9,8},{10,11... | collective-permute-start | bytes 1499144 | tf_op jit(solution)/shard_map/cond/branch_29_fun/ppermute | solution.py:423
  10.2 1.3 %collective-permute-start.50 = (bf16[1952,128]{1,0:T(8,128)(2,1)S(1)}, bf16[1952,128]{1,0:T(8,128)(2,1)S(1)}, u32[]{:S(2)}, u32[]{:S(2)}) collective-permute-start(bf16[1952,128]{1,0:T(8,128)(2,1)S(1)} %get-tuple-element.1011), channel_id=1, source_target_pairs={{257,0},{259,2},{261,4},{263,6},{265,8},{267,10},{269,12},{271,14}... | collective-permute-start | bytes 1499144 | tf_op jit(solution)/shard_map/cond/branch_29_fun/ppermute | solution.py:423
  11.5 0.0 collective-permute-done.49
  11.5 23.9 %collective-permute-done.50 = bf16[1952,128]{1,0:T(8,128)(2,1)S(1)} collective-permute-done((bf16[1952,128]{1,0:T(8,128)(2,1)S(1)}, bf16[1952,128]{1,0:T(8,128)(2,1)S(1)}, u32[]{:S(2)}, u32[]{:S(2)}) %collective-permute-start.50) | collective-permute-done | bytes 499744 | tf_op jit(solution)/shard_map/cond/branch_29_fun/ppermute | solution.py:423
  35.4 0.1 select_select_fusion.28
  35.8 1.7 %place_rows.1 = (bf16[128,3584]{1,0:T(8,128)(2,1)}, bf16[128,3584]{1,0:T(8,128)(2,1)}, bf16[128,512]{1,0:T(8,128)(2,1)}, bf16[128,512]{1,0:T(8,128)(2,1)}) custom-call(s32[4,1,128]{2,1,0:T(1,128)S(1)} %get-tuple-element.846.facts_ref, ...), custom_call_target="tpu_custom_call", output_to_operand_aliasing={{0}: (2, {}), {1}: (3, {}), {2}: (4, {}), {3}: (5, {})} | custom-call | flops 234881024 | bytes 2097152 | tf_op jit(solution)/shard_map/place_rows/pallas_call | solution.py:360
  (2 shorter events, 0.0 us)
Async XLA Ops:
  3.9 5.3 %collective-permute-start.117 = (bf16[1952,128]{1,0:T(8,128)(2,1)S(1)}, bf16[1952,128]{1,0:T(8,128)(2,1)S(1)}, u32[]{:S(2)}, u32[]{:S(2)}) collective-permute-start(bf16[1952,128]{1,0:T(8,128)(2,1)S(1)} %get-tuple-element.848), channel_id=1, source_target_pairs={{0,8},{8,0},{16,24},{24,16},{32,40},{40,32},{48,56},{56,48},{64,72... | collective-permute-start | bytes 1499144 | tf_op jit(solution)/shard_map/ppermute | solution.py:403
  9.5 2.0 %collective-permute-start.49 = (bf16[1952,128]{1,0:T(8,128)(2,1)S(1)}, bf16[1952,128]{1,0:T(8,128)(2,1)S(1)}, u32[]{:S(2)}, u32[]{:S(2)}) collective-permute-start(bf16[1952,128]{1,0:T(8,128)(2,1)S(1)} %get-tuple-element.1012), channel_id=1, source_target_pairs={{0,1},{1,0},{2,3},{3,2},{4,5},{5,4},{6,7},{7,6},{8,9},{9,8},{10,11... | collective-permute-start | bytes 1499144 | tf_op jit(solution)/shard_map/cond/branch_29_fun/ppermute | solution.py:423
  10.2 25.2 %collective-permute-start.50 = (bf16[1952,128]{1,0:T(8,128)(2,1)S(1)}, bf16[1952,128]{1,0:T(8,128)(2,1)S(1)}, u32[]{:S(2)}, u32[]{:S(2)}) collective-permute-start(bf16[1952,128]{1,0:T(8,128)(2,1)S(1)} %get-tuple-element.1011), channel_id=1, source_target_pairs={{257,0},{259,2},{261,4},{263,6},{265,8},{267,10},{269,12},{271,14}... | collective-permute-start | bytes 1499144 | tf_op jit(solution)/shard_map/cond/branch_29_fun/ppermute | solution.py:423

commit v3 on v2

v3 whole, which is shorter than its diff:
```python
import functools

import jax
import jax.numpy as jnp
from jax import lax
from jax.experimental import pallas as pl
from jax.experimental.pallas import tpu as pltpu
from jax.sharding import PartitionSpec as P

HD = 128
KVH = 4
GROUP = 7
BLOCK = 64
SEQ = 2 * BLOCK
SCALE = 1.0 / HD**0.5
PAIR = 2 * GROUP * HD
TRI = GROUP * BLOCK
DIAG = 16
SIDE = 2 * BLOCK
ROWS = TRI + DIAG + 4 * SIDE
AT = TRI + DIAG
VMEM_LIMIT = 40 * 1024 * 1024

NT = (((1,), (1,)), ((), ()))
NN = (((1,), (0,)), ((), ()))
TN = (((0,), (0,)), ((), ()))


def mm(a, b, dims):
    return lax.dot_general(a, b, dims, preferred_element_type=jnp.float32)


def iota(shape, dim):
    return lax.broadcasted_iota(jnp.int32, shape, dim)


def fold_matrix():
    shape = (BLOCK, 2 * BLOCK)
    return jnp.where((iota(shape, 1) & (BLOCK - 1)) == iota(shape, 0), 1.0, 0.0).astype(jnp.bfloat16)


def turn(fold, pair):
    low = iota(pair.shape, 1) < BLOCK
    zero = jnp.zeros_like(pair)
    split = jnp.concatenate([jnp.where(low, pair, zero), jnp.where(low, zero, pair)], 0)
    return mm(fold, split, NT)


def read_moves(plan_ref, near, core, far):
    me = lax.axis_index("dp") * core + lax.axis_index("fsdp")
    base = me & ~(near + far)
    z, c = [], []
    for q in range(4):
        at = base + (q & 1) * near + (q >> 1) * far
        c.append(plan_ref[1, 1, at])
        z.append(plan_ref[0, 1, at ^ (c[q] * core)])
    y = [plan_ref[2, 1, base], plan_ref[2, 1, base + near]]
    here = ((me // near) & 1) + 2 * ((me // far) & 1)

    def pick(values, index):
        out = values[0]
        for i in range(1, len(values)):
            out = jnp.where(index == i, values[i], out)
        return out

    def origin(chip):
        crossed = pick(y, chip & 1)
        passed = chip ^ (2 * crossed)
        return pick(z, passed) ^ (2 * crossed), pick(c, passed)

    branch = y[0] + 2 * y[1] + 4 * z[0] + 8 * z[1] + 16 * z[2] + 32 * z[3]
    send = [origin(here ^ step)[1] for step in range(1, 4)]
    mine, other = origin(here)
    take = jnp.where(mine == 0, other, mine + 1)

    return branch, send, take


def fill_zeros(full):
    zero = jnp.zeros((BLOCK, HD), jnp.bfloat16)
    for h in range(GROUP):
        r = h * 2 * BLOCK
        full[r : r + BLOCK, HD:] = zero
        full[r + BLOCK : r + 2 * BLOCK, 0:HD] = zero


def fill_pair(full, rows):
    for h in range(GROUP):
        r = h * 2 * BLOCK
        full[r : r + BLOCK, 0:HD] = rows[:, h * HD : (h + 1) * HD]
        full[r + BLOCK : r + 2 * BLOCK, HD:] = rows[:, (GROUP + h) * HD : (GROUP + h + 1) * HD]


def attend(q, k, v, g, allow):
    score = jnp.where(allow, mm(k, q, NT) * SCALE, -1e30)
    weights = jnp.exp(score - jnp.max(score, axis=0, keepdims=True))
    probs = weights * (1.0 / jnp.sum(weights, axis=0, keepdims=True))
    probs_b = probs.astype(jnp.bfloat16)
    dprob = mm(v, g, NT)
    delta = jnp.sum(probs * dprob, axis=0, keepdims=True)
    dscore = (probs * (dprob - delta) * SCALE).astype(jnp.bfloat16)
    dv = mm(probs_b, g, NN).astype(jnp.bfloat16)
    dk = mm(dscore, q, NN).astype(jnp.bfloat16)
    return probs_b, dscore, dk, dv


def block_mask(live):
    wide = (BLOCK, GROUP * 2 * BLOCK)
    key_pos = iota(wide, 0)
    query_pos = iota(wide, 1) & (BLOCK - 1)
    return (key_pos <= query_pos) & (key_pos < live)


def pack_kernel(bits, first_hbm, valid_hbm, plan_hbm, q_hbm, k_hbm, v_hbm, g_hbm, *refs):
    pack_ref, send_ref, facts_ref = refs[:3]
    first_ref, valid_ref, plan_ref, qbd, gbd, sem = refs[3:9]
    bufs = refs[9:]
    q_buf, k_buf, v_buf, g_buf = bufs
    words = [
        pltpu.make_async_copy(hbm, ref, sem.at[2, i])
        for i, (hbm, ref) in enumerate(
            ((plan_hbm, plan_ref), (valid_hbm, valid_ref), (first_hbm, first_ref))
        )
    ]
    copies = []
    for chunk in range(2):
        for i, (hbm, buf) in enumerate(zip((q_hbm, k_hbm, v_hbm, g_hbm), bufs)):
            width = buf.shape[1] // 2
            cut = pl.ds(chunk * width, width)
            copies.append(
                pltpu.make_async_copy(
                    hbm.at[pl.ds(BLOCK, BLOCK), cut], buf.at[:, cut], sem.at[chunk, i]
                )
            )
    for c in words + copies:
        c.start()
    for chunk in range(2):
        fill_zeros(qbd.at[chunk])
        fill_zeros(gbd.at[chunk])
    for c in words:
        c.wait()
    branch, send, take = read_moves(plan_ref, *bits)
    me = lax.axis_index("dp") * bits[1] + lax.axis_index("fsdp")
    for i in range(3):
        send_ref[i] = jnp.full((1, HD), send[i], jnp.int32)
    facts = (take, jnp.where(first_ref[1, me] == 0, 1, 0), valid_ref[0, me], valid_ref[1, me], branch)
    for i, fact in enumerate(facts):
        facts_ref[i] = jnp.full((1, HD), fact, jnp.int32)
    allow = block_mask(valid_ref[1, me])
    fold = fold_matrix()
    square = (BLOCK, 2 * BLOCK)
    row, lane = iota(square, 0), iota(square, 1) & (BLOCK - 1)
    for c in copies:
        c.wait()
    for chunk in range(2):
        base = chunk * ROWS
        heads = slice(chunk * PAIR, (chunk + 1) * PAIR)
        pair = slice(chunk * 2 * HD, (chunk + 1) * 2 * HD)
        fill_pair(qbd.at[chunk], q_buf.at[:, heads])
        fill_pair(gbd.at[chunk], g_buf.at[:, heads])
        k, v = k_buf[:, pair], v_buf[:, pair]
        probs_b, dscore, dk, dv = attend(qbd[chunk], k, v, gbd[chunk], allow)
        diag = []
        for h in range(GROUP):
            cut = slice(h * 2 * BLOCK, (h + 1) * 2 * BLOCK)
            ds = dscore[:, cut]
            pack_ref[base + h * BLOCK : base + (h + 1) * BLOCK, :] = jnp.where(
                row <= lane, probs_b[:, cut].astype(jnp.float32), turn(fold, ds)
            ).astype(jnp.bfloat16)
            diag.append(
                jnp.sum(jnp.where(row == lane, ds.astype(jnp.float32), 0.0), axis=0, keepdims=True)
            )
        diag.append(jnp.zeros((DIAG - GROUP, 2 * BLOCK), jnp.float32))
        pack_ref[base + TRI : base + AT, :] = jnp.concatenate(diag, 0).astype(jnp.bfloat16)
        for i, part in enumerate((k, v, dk, dv)):
            for j in range(2):
                r = base + AT + i * SIDE + j * BLOCK
                pack_ref[r : r + BLOCK, :] = part[:, j * HD : (j + 1) * HD]


def make_pack(bits, first, valid, plan, q, k, v, g):
    hbm = pl.BlockSpec(memory_space=pltpu.HBM)
    vmem = pl.BlockSpec(memory_space=pltpu.VMEM)
    return pl.pallas_call(
        functools.partial(pack_kernel, bits),
        out_shape=[
            pltpu.VMEM((2 * ROWS, HD), jnp.bfloat16),
            pltpu.VMEM((3, 1, HD), jnp.int32),
            pltpu.VMEM((5, 1, HD), jnp.int32),
        ],
        in_specs=[hbm] * 7,
        out_specs=[vmem] * 3,
        scratch_shapes=[
            pltpu.SMEM(first.shape, jnp.int32),
            pltpu.SMEM(valid.shape, jnp.int32),
            pltpu.SMEM(plan.shape, jnp.int32),
            pltpu.VMEM((2, GROUP * 2 * BLOCK, 2 * HD), jnp.bfloat16),
            pltpu.VMEM((2, GROUP * 2 * BLOCK, 2 * HD), jnp.bfloat16),
            pltpu.SemaphoreType.DMA((3, 4)),
        ]
        + [pltpu.VMEM((BLOCK, x.shape[1]), x.dtype) for x in (q, k, v, g)],
        compiler_params=pltpu.CompilerParams(vmem_limit_bytes=VMEM_LIMIT),
        cost_estimate=pl.CostEstimate(
            flops=16 * BLOCK * GROUP * 2 * BLOCK * 2 * HD, bytes_accessed=3 << 20, transcendentals=0
        ),
        name="pack_rows",
    )(*(pltpu.with_memory_space_constraint(x, pltpu.HBM) for x in (first, valid, plan, q, k, v, g)))


def finish_kernel(facts_ref, pack, q_hbm, k_hbm, v_hbm, g_hbm, *refs):
    outs, ins, news = refs[:4], refs[4:8], refs[8:12]
    qbd, gbd, in_sem, out_sem = refs[12:]
    q_buf, k_buf, v_buf, g_buf = ins
    o_buf, dq_buf, dk_buf, dv_buf = news
    joined = jnp.max(facts_ref[1]) == 1

    def read(block):
        rows = pl.ds(block * BLOCK, BLOCK)
        return [
            pltpu.make_async_copy(hbm.at[rows, :], buf.at[rows, :], in_sem.at[block, i])
            for i, (hbm, buf) in enumerate(zip((q_hbm, k_hbm, v_hbm, g_hbm), ins))
        ]

    def write(block, part, parts):
        copies = []
        for i, (buf, out) in enumerate(zip(news, outs)):
            width = buf.shape[1] // parts
            at = (pl.ds(block * BLOCK, BLOCK), pl.ds(part * width, width))
            copies.append(
                pltpu.make_async_copy(buf.at[at], out.at[at], out_sem.at[2 * block + part, i])
            )
            copies[-1].start()
        return copies

    low, high = read(0), read(1)
    for c in low:
        c.start()

    @pl.when(joined)
    def _():
        for c in high:
            c.start()

    @pl.when(jnp.logical_not(joined))
    def _():
        fold = fold_matrix()
        square = (BLOCK, 2 * BLOCK)
        row, lane = iota(square, 0), iota(square, 1) & (BLOCK - 1)
        zero = jnp.zeros((BLOCK, HD), jnp.bfloat16)
        copies = []
        for chunk in range(2):
            fill_zeros(qbd.at[chunk])
            fill_zeros(gbd.at[chunk])
        for chunk in range(2):
            base = chunk * ROWS

            def spread(i):
                r = base + AT + i * SIDE
                return jnp.concatenate(
                    [
                        jnp.concatenate([pack[r : r + BLOCK, :], zero], 1),
                        jnp.concatenate([zero, pack[r + BLOCK : r + SIDE, :]], 1),
                    ],
                    0,
                )

            kbd, vbd = spread(0), spread(1)
            for j in range(2):
                for i, buf in ((2, dk_buf), (3, dv_buf)):
                    r, at = base + AT + i * SIDE + j * BLOCK, (2 * chunk + j) * HD
                    buf[BLOCK:, at : at + HD] = pack[r : r + BLOCK, :]
            diag = pack[base + TRI : base + AT, :].astype(jnp.float32)
            probs, dscore = [], []
            for h in range(GROUP):
                both = pack[base + h * BLOCK : base + (h + 1) * BLOCK, :].astype(jnp.float32)
                upper = jnp.where(row <= lane, both, 0.0).astype(jnp.bfloat16)
                probs.append(turn(fold, upper).astype(jnp.bfloat16))
                line = jnp.where(row == lane, diag[h : h + 1, :], 0.0)
                dscore.append(jnp.where(row > lane, both, line).astype(jnp.bfloat16))
            out = mm(jnp.concatenate(probs, 0), vbd, NN).astype(jnp.bfloat16)
            dq = mm(jnp.concatenate(dscore, 0), kbd, NN).astype(jnp.bfloat16)
            for buf, val in ((o_buf, out), (dq_buf, dq)):
                for h in range(GROUP):
                    for j in range(2):
                        at = chunk * PAIR + (j * GROUP + h) * HD
                        buf[BLOCK:, at : at + HD] = val[
                            h * BLOCK : (h + 1) * BLOCK, j * HD : (j + 1) * HD
                        ]
        copies += write(1, 0, 1)
        for c in low:
            c.wait()
        allow = block_mask(jnp.max(facts_ref[2]))
        for chunk in range(2):
            heads = slice(chunk * PAIR, (chunk + 1) * PAIR)
            pair = slice(chunk * 2 * HD, (chunk + 1) * 2 * HD)
            fill_pair(qbd.at[chunk], q_buf.at[0:BLOCK, heads])
            fill_pair(gbd.at[chunk], g_buf.at[0:BLOCK, heads])
            k, v = k_buf[0:BLOCK, pair], v_buf[0:BLOCK, pair]
            probs_b, dscore, dk, dv = attend(qbd[chunk], k, v, gbd[chunk], allow)
            dk_buf[0:BLOCK, pair] = dk
            dv_buf[0:BLOCK, pair] = dv
            for buf, squares, other in ((o_buf, probs_b, v), (dq_buf, dscore, k)):
                val = mm(squares, other, TN).astype(jnp.bfloat16)
                for h in range(GROUP):
                    for j in range(2):
                        r, at = (2 * h + j) * BLOCK, chunk * PAIR + (j * GROUP + h) * HD
                        buf[0:BLOCK, at : at + HD] = val[r : r + BLOCK, j * HD : (j + 1) * HD]
            copies += write(0, chunk, 2)
        for c in copies:
            c.wait()

    @pl.when(joined)
    def _():
        for c in low + high:
            c.wait()
        wide = (SEQ, GROUP * SEQ)
        key_pos = iota(wide, 0)
        query_pos = iota(wide, 1) & (SEQ - 1)
        live_of = jnp.where(key_pos < BLOCK, jnp.max(facts_ref[2]), jnp.max(facts_ref[3]))
        allow = (key_pos <= query_pos) & ((key_pos & (BLOCK - 1)) < live_of)

        @pl.loop(0, KVH)
        def _(i):
            one = pl.ds(pl.multiple_of(i * HD, HD), HD)

            def head(h):
                return pl.ds(pl.multiple_of((i * GROUP + h) * HD, HD), HD)

            k, v = k_buf[:, one], v_buf[:, one]
            q = jnp.concatenate([q_buf[:, head(h)] for h in range(GROUP)], 0)
            g = jnp.concatenate([g_buf[:, head(h)] for h in range(GROUP)], 0)
            probs_b, dscore, dk, dv = attend(q, k, v, g, allow)
            dk_buf[:, one] = dk
            dv_buf[:, one] = dv
            for h in range(GROUP):
                cut = slice(h * SEQ, (h + 1) * SEQ)
                o_buf[:, head(h)] = mm(probs_b[:, cut], v, TN).astype(jnp.bfloat16)
                dq_buf[:, head(h)] = mm(dscore[:, cut], k, TN).astype(jnp.bfloat16)

        for c in write(0, 0, 1) + write(1, 0, 1):
            c.wait()


def finish(facts, pack, q, k, v, g):
    vmem = pl.BlockSpec(memory_space=pltpu.VMEM)
    hbm = pl.BlockSpec(memory_space=pltpu.HBM)
    return pl.pallas_call(
        finish_kernel,
        out_shape=[jax.ShapeDtypeStruct(x.shape, jnp.bfloat16) for x in (q, q, k, v)],
        in_specs=[vmem] * 2 + [hbm] * 4,
        out_specs=[hbm] * 4,
        scratch_shapes=[pltpu.VMEM(x.shape, jnp.bfloat16) for x in (q, k, v, g, q, q, k, v)]
        + [pltpu.VMEM((2, GROUP * 2 * BLOCK, 2 * HD), jnp.bfloat16)] * 2
        + [pltpu.SemaphoreType.DMA((2, 4)), pltpu.SemaphoreType.DMA((4, 4))],
        compiler_params=pltpu.CompilerParams(vmem_limit_bytes=VMEM_LIMIT),
        cost_estimate=pl.CostEstimate(
            flops=12 * KVH * GROUP * SEQ * SEQ * HD, bytes_accessed=4 << 20, transcendentals=0
        ),
        name="finish_rows",
    )(facts, pack, *(pltpu.with_memory_space_constraint(x, pltpu.HBM) for x in (q, k, v, g)))


def origins(branch):
    found = []
    for chip in range(4):
        crossed = branch >> (chip & 1) & 1
        passed = chip ^ 2 * crossed
        found.append(2 * crossed ^ (branch >> 2 + passed & 1))
    return found


def body(queries, keys, values, out_grad, doc_first, doc_valid, move_plan):
    core, dp = lax.axis_size("fsdp"), lax.axis_size("dp")
    near, far = 1, core * dp // 2
    bits = (near, core, far)
    args = (queries, keys, values, out_grad)
    first, valid, plan = doc_first.T, doc_valid.T, jnp.swapaxes(move_plan, 1, 2)
    pack, send, facts = make_pack(bits, first, valid, plan, *args)
    other = lax.ppermute(pack, "dp", [(i, i ^ 1) for i in range(dp)])

    def route(index):
        found = origins(index)

        def run(pack, other, send, facts):
            take = facts[0]
            got = []
            for step in (1, 2, 3):
                if step not in found:
                    continue
                chips = [chip for chip in range(4) if found[chip] == step]
                if len(chips) == 3:
                    chips = [0, 1, 2, 3]
                pairs = []
                for i in range(core * dp):
                    if i // near % 2 + 2 * (i // far % 2) in chips:
                        pairs.append((i ^ (step & 1) * near ^ (step >> 1) * far, i))
                sent = jnp.where(send[step - 1] == 1, other, pack)
                got.append((step, lax.ppermute(sent, ("dp", "fsdp"), pairs)))
            result = jnp.where(take == 1, other, pack)
            for step, rows in got:
                result = jnp.where(take == step + 1, rows, result)
            return result

        return run

    rows = lax.switch(facts[4, 0, 0], [route(i) for i in range(64)], pack, other, send, facts)
    return tuple(finish(facts, rows, *args))


def solution(mesh):
    rows = P(("dp", "fsdp"), None)
    return jax.shard_map(
        body,
        mesh=mesh,
        in_specs=(rows,) * 4 + (P(),) * 3,
        out_specs=(rows,) * 4,
        check_vma=False,
    )
```

time: 38 us -> 43.5 us (1.14)
  the two profiles are of different devices: /device:TPU:432 before, /device:TPU:436 now
where the time goes in v3:
time: 43.5 us; the launch traced here: 43.3 us
  waiting for transfers between devices  21.6 us (50%)
  starting transfers between devices  12.6 us (29%)
  Pallas kernels  6.35 us (15%)
  between operations  1.49 us (3%)
  local copies, waits for them, and re-layouts  0.51 us (1%)
  loops' own time  0.46 us (1%)
    ppermute x2, waiting for transfers between devices, run(): got.append((step, lax.ppermute(sent, ('dp', 'fsdp'), pairs)))  21 us
    ppermute x2, starting transfers between devices, run(): got.append((step, lax.ppermute(sent, ('dp', 'fsdp'), pairs)))  10.7 us
    pallas_call x1, Pallas kernels, finish(): pl.pallas_call(finish_kernel, out_shape=[jax.ShapeDtypeStruct(x.shape, jn...  3.65 us
    pallas_call x1, Pallas kernels, make_pack(): pl.pallas_call(functools.partial(pack_kernel, bits), out_shape=[pltpu.VME...  2.7 us
    ppermute x1, starting transfers between devices, body(): other = lax.ppermute(pack, 'dp', [(i, i ^ 1) for i in range(dp)])  1.92 us
  transfers between devices with their start and end apart: 3, of which 2 were waited for; matrix products, arithmetic and copies ran while one was open for 1% of the time, Pallas kernels for 0%

profile of v3, /device:TPU:436, one launch (start us, length us, event | category | flops | bytes accessed | tf_op | source)
XLA Modules:
  0.0 43.3 jit_solution(1903774438975240737)
XLA Ops:
  0.6 2.7 %pack_rows.1 = (bf16[1952,128]{1,0:T(8,128)(2,1)S(1)}, s32[3,1,128]{2,1,0:T(1,128)S(1)}, s32[5,1,128]{2,1,0:T(1,128)S(1)}) custom-call(s32[2,512]{1,0:T(2,128)} %bitcast.601, s32[2,512]{1,0:T(2,128)} %bitcast.602, s32[3,2,512]{2,1,0:T(2,128)} %bitcast.600, bf16[128,3584]{1,0:T(8,128)(2,1)} %q_hbm.3, bf16[128,512]{1,0:T(8,128)(2,1)} %k_hbm.3, ...), custom_call_target="tpu_custom_call" | custom-call | flops 234881024 | bytes 3145728 | tf_op jit(solution)/shard_map/pack_rows/pallas_call | solution.py:184
  3.3 1.9 %collective-permute-start.117 = (bf16[1952,128]{1,0:T(8,128)(2,1)S(1)}, bf16[1952,128]{1,0:T(8,128)(2,1)S(1)}, u32[]{:S(2)}, u32[]{:S(2)}) collective-permute-start(bf16[1952,128]{1,0:T(8,128)(2,1)S(1)} %get-tuple-element.838), channel_id=1, source_target_pairs={{0,8},{8,0},{16,24},{24,16},{32,40},{40,32},{48,56},{56,48},{64,72... | collective-permute-start | bytes 1499144 | tf_op jit(solution)/shard_map/ppermute | solution.py:379
  5.3 0.5 %slice.546 = s32[1,1,1]{2,1,0:T(1,128)} slice(s32[5,1,128]{2,1,0:T(1,128)S(1)} %get-tuple-element.837.facts_ref), slice={[4:5], [0:1], [0:1]} | slice | bytes 8 | tf_op jit(solution)/shard_map/slice | solution.py:406
  6.4 0.7 %collective-permute-done.117 = bf16[1952,128]{1,0:T(8,128)(2,1)S(1)} collective-permute-done((bf16[1952,128]{1,0:T(8,128)(2,1)S(1)}, bf16[1952,128]{1,0:T(8,128)(2,1)S(1)}, u32[]{:S(2)}, u32[]{:S(2)}) %collective-permute-start.117) | collective-permute-done | bytes 499744 | tf_op jit(solution)/shard_map/ppermute | solution.py:379
  7.1 32.3 %conditional.1 = (bf16[1952,128]{1,0:T(8,128)(2,1)S(1)}) conditional(s32[]{:T(128)} %bitcast.301, (s32[5,1,128]{2,1,0:T(1,128)S(1)}, bf16[1952,128]{1,0:T(8,128)(2,1)S(1)}, bf16[1952,128]{1,0:T(8,128)(2,1)S(1)}) %tuple.199, (s32[5,1,128]{2,1,0:T(1,128)S(1)}, s32[3,1,128]{2,1,0:T(1,128)S(1)}, ...), branch_computations={%region_0.1_spmd, %region_1.2_spmd, %region_2.3_spmd, %region_3.4_... | conditional | flops 1749888 | bytes 11497344 | solution.py:406
  7.1 0.1 broadcast_select_fusion.16
  7.2 0.7 %collective-permute-start.15 = (bf16[1952,128]{1,0:T(8,128)(2,1)S(1)}, bf16[1952,128]{1,0:T(8,128)(2,1)S(1)}, u32[]{:S(2)}, u32[]{:S(2)}) collective-permute-start(bf16[1952,128]{1,0:T(8,128)(2,1)S(1)} %get-tuple-element.886), channel_id=1, source_target_pairs={{0,257},{2,259},{4,261},{6,263},{8,265},{10,267},{12,269},{14,271}... | collective-permute-start | bytes 1499144 | tf_op jit(solution)/shard_map/cond/branch_11_fun/ppermute | solution.py:398
  7.9 10.0 %collective-permute-start.16 = (bf16[1952,128]{1,0:T(8,128)(2,1)S(1)}, bf16[1952,128]{1,0:T(8,128)(2,1)S(1)}, u32[]{:S(2)}, u32[]{:S(2)}) collective-permute-start(bf16[1952,128]{1,0:T(8,128)(2,1)S(1)} %get-tuple-element.885), channel_id=1, source_target_pairs={{256,0},{257,1},{258,2},{259,3},{260,4},{261,5},{262,6},{263,7},{2... | collective-permute-start | bytes 1499144 | tf_op jit(solution)/shard_map/cond/branch_11_fun/ppermute | solution.py:398
  17.9 0.0 collective-permute-done.15
  17.9 21.0 %collective-permute-done.16 = bf16[1952,128]{1,0:T(8,128)(2,1)S(1)} collective-permute-done((bf16[1952,128]{1,0:T(8,128)(2,1)S(1)}, bf16[1952,128]{1,0:T(8,128)(2,1)S(1)}, u32[]{:S(2)}, u32[]{:S(2)}) %collective-permute-start.16) | collective-permute-done | bytes 499744 | tf_op jit(solution)/shard_map/cond/branch_11_fun/ppermute | solution.py:398
  38.9 0.1 select_select_fusion.10
  39.4 3.7 %finish_rows.1 = (bf16[128,3584]{1,0:T(8,128)(2,1)}, bf16[128,3584]{1,0:T(8,128)(2,1)}, bf16[128,512]{1,0:T(8,128)(2,1)}, bf16[128,512]{1,0:T(8,128)(2,1)}) custom-call(s32[5,1,128]{2,1,0:T(1,128)S(1)} %get-tuple-element.837.facts_ref, bf16[1952,128]{1,0:T(8,128)(2,1)S(1)} %get-tuple-element.1212.pack, bf16[128,3584]{1,0:T(8,128)(2,1)} %q_hbm.3, ...), custom_call_target="tpu_custom_call" | custom-call | flops 704643072 | bytes 4194304 | tf_op jit(solution)/shard_map/finish_rows/pallas_call | solution.py:347
  (2 shorter events, 0.0 us)
Async XLA Ops:
  3.3 3.8 %collective-permute-start.117 = (bf16[1952,128]{1,0:T(8,128)(2,1)S(1)}, bf16[1952,128]{1,0:T(8,128)(2,1)S(1)}, u32[]{:S(2)}, u32[]{:S(2)}) collective-permute-start(bf16[1952,128]{1,0:T(8,128)(2,1)S(1)} %get-tuple-element.838), channel_id=1, source_target_pairs={{0,8},{8,0},{16,24},{24,16},{32,40},{40,32},{48,56},{56,48},{64,72... | collective-permute-start | bytes 1499144 | tf_op jit(solution)/shard_map/ppermute | solution.py:379
  7.2 10.7 %collective-permute-start.15 = (bf16[1952,128]{1,0:T(8,128)(2,1)S(1)}, bf16[1952,128]{1,0:T(8,128)(2,1)S(1)}, u32[]{:S(2)}, u32[]{:S(2)}) collective-permute-start(bf16[1952,128]{1,0:T(8,128)(2,1)S(1)} %get-tuple-element.886), channel_id=1, source_target_pairs={{0,257},{2,259},{4,261},{6,263},{8,265},{10,267},{12,269},{14,271}... | collective-permute-start | bytes 1499144 | tf_op jit(solution)/shard_map/cond/branch_11_fun/ppermute | solution.py:398
  7.9 31.0 %collective-permute-start.16 = (bf16[1952,128]{1,0:T(8,128)(2,1)S(1)}, bf16[1952,128]{1,0:T(8,128)(2,1)S(1)}, u32[]{:S(2)}, u32[]{:S(2)}) collective-permute-start(bf16[1952,128]{1,0:T(8,128)(2,1)S(1)} %get-tuple-element.885), channel_id=1, source_target_pairs={{256,0},{257,1},{258,2},{259,3},{260,4},{261,5},{262,6},{263,7},{2... | collective-permute-start | bytes 1499144 | tf_op jit(solution)/shard_map/cond/branch_11_fun/ppermute | solution.py:398

commit v4 on v3

--- a/solution.py
+++ b/solution.py
@@ -150,9 +150,9 @@
     fold = fold_matrix()
     square = (BLOCK, 2 * BLOCK)
     row, lane = iota(square, 0), iota(square, 1) & (BLOCK - 1)
-    for c in copies:
-        c.wait()
     for chunk in range(2):
+        for c in copies[4 * chunk : 4 * chunk + 4]:
+            c.wait()
         base = chunk * ROWS
         heads = slice(chunk * PAIR, (chunk + 1) * PAIR)
         pair = slice(chunk * 2 * HD, (chunk + 1) * 2 * HD)
@@ -286,7 +286,7 @@
                         buf[BLOCK:, at : at + HD] = val[
                             h * BLOCK : (h + 1) * BLOCK, j * HD : (j + 1) * HD
                         ]
-        copies += write(1, 0, 1)
+            copies += write(1, chunk, 2)
         for c in low:
             c.wait()
         allow = block_mask(jnp.max(facts_ref[2]))
@@ -300,11 +300,13 @@
             dk_buf[0:BLOCK, pair] = dk
             dv_buf[0:BLOCK, pair] = dv
             for buf, squares, other in ((o_buf, probs_b, v), (dq_buf, dscore, k)):
-                val = mm(squares, other, TN).astype(jnp.bfloat16)
-                for h in range(GROUP):
-                    for j in range(2):
-                        r, at = (2 * h + j) * BLOCK, chunk * PAIR + (j * GROUP + h) * HD
-                        buf[0:BLOCK, at : at + HD] = val[r : r + BLOCK, j * HD : (j + 1) * HD]
+                turned = squares.T
+                for j in range(2):
+                    rows = [turned[(2 * h + j) * BLOCK : (2 * h + j + 1) * BLOCK] for h in range(GROUP)]
+                    val = mm(jnp.concatenate(rows, 0), other[:, j * HD : (j + 1) * HD], NN).astype(jnp.bfloat16)
+                    for h in range(GROUP):
+                        at = chunk * PAIR + (j * GROUP + h) * HD
+                        buf[0:BLOCK, at : at + HD] = val[h * BLOCK : (h + 1) * BLOCK]
             copies += write(0, chunk, 2)
         for c in copies:
             c.wait()

time: 43.5 us -> 37.5 us (0.86)
  the two profiles are of different devices: /device:TPU:436 before, /device:TPU:282 now
where the time goes in v4:
time: 37.5 us; the launch traced here: 37.3 us
  waiting for transfers between devices  17.6 us (47%)
  starting transfers between devices  11.1 us (30%)
  Pallas kernels  6.02 us (16%)
  between operations  1.49 us (4%)
  local copies, waits for them, and re-layouts  0.51 us (1%)
    ppermute x3, waiting for transfers between devices, run(): got.append((step, lax.ppermute(sent, ('dp', 'fsdp'), pairs)))  16.9 us
    ppermute x3, starting transfers between devices, run(): got.append((step, lax.ppermute(sent, ('dp', 'fsdp'), pairs)))  9.15 us
    pallas_call x1, Pallas kernels, finish(): pl.pallas_call(finish_kernel, out_shape=[jax.ShapeDtypeStruct(x.shape, jn...  3.42 us
    pallas_call x1, Pallas kernels, make_pack(): pl.pallas_call(functools.partial(pack_kernel, bits), out_shape=[pltpu.VME...  2.6 us
    ppermute x1, starting transfers between devices, body(): other = lax.ppermute(pack, 'dp', [(i, i ^ 1) for i in range(dp)])  1.92 us
  transfers between devices with their start and end apart: 4, of which 2 were waited for; matrix products, arithmetic and copies ran while one was open for 1% of the time, Pallas kernels for 0%

profile of v4, /device:TPU:282, one launch (start us, length us, event | category | flops | bytes accessed | tf_op | source)
XLA Modules:
  0.0 37.3 jit_solution(16357774548246483034)
XLA Ops:
  0.6 2.6 %pack_rows.1 = (bf16[1952,128]{1,0:T(8,128)(2,1)S(1)}, s32[3,1,128]{2,1,0:T(1,128)S(1)}, s32[5,1,128]{2,1,0:T(1,128)S(1)}) custom-call(s32[2,512]{1,0:T(2,128)} %bitcast.601, s32[2,512]{1,0:T(2,128)} %bitcast.602, s32[3,2,512]{2,1,0:T(2,128)} %bitcast.600, bf16[128,3584]{1,0:T(8,128)(2,1)} %q_hbm.3, bf16[128,512]{1,0:T(8,128)(2,1)} %k_hbm.3, ...), custom_call_target="tpu_custom_call" | custom-call | flops 234881024 | bytes 3145728 | tf_op jit(solution)/shard_map/pack_rows/pallas_call | solution.py:184
  3.2 1.9 %collective-permute-start.117 = (bf16[1952,128]{1,0:T(8,128)(2,1)S(1)}, bf16[1952,128]{1,0:T(8,128)(2,1)S(1)}, u32[]{:S(2)}, u32[]{:S(2)}) collective-permute-start(bf16[1952,128]{1,0:T(8,128)(2,1)S(1)} %get-tuple-element.838), channel_id=1, source_target_pairs={{0,8},{8,0},{16,24},{24,16},{32,40},{40,32},{48,56},{56,48},{64,72... | collective-permute-start | bytes 1499144 | tf_op jit(solution)/shard_map/ppermute | solution.py:381
  5.2 0.5 %slice.546 = s32[1,1,1]{2,1,0:T(1,128)} slice(s32[5,1,128]{2,1,0:T(1,128)S(1)} %get-tuple-element.837.facts_ref), slice={[4:5], [0:1], [0:1]} | slice | bytes 8 | tf_op jit(solution)/shard_map/slice | solution.py:408
  6.3 0.7 %collective-permute-done.117 = bf16[1952,128]{1,0:T(8,128)(2,1)S(1)} collective-permute-done((bf16[1952,128]{1,0:T(8,128)(2,1)S(1)}, bf16[1952,128]{1,0:T(8,128)(2,1)S(1)}, u32[]{:S(2)}, u32[]{:S(2)}) %collective-permute-start.117) | collective-permute-done | bytes 499744 | tf_op jit(solution)/shard_map/ppermute | solution.py:381
  7.0 26.6 %conditional.1 = (bf16[1952,128]{1,0:T(8,128)(2,1)S(1)}) conditional(s32[]{:T(128)} %bitcast.301, (s32[5,1,128]{2,1,0:T(1,128)S(1)}, bf16[1952,128]{1,0:T(8,128)(2,1)S(1)}, bf16[1952,128]{1,0:T(8,128)(2,1)S(1)}) %tuple.199, (s32[5,1,128]{2,1,0:T(1,128)S(1)}, s32[3,1,128]{2,1,0:T(1,128)S(1)}, ...), branch_computations={%region_0.1_spmd, %region_1.2_spmd, %region_2.3_spmd, %region_3.4_... | conditional | flops 1749888 | bytes 11497344 | solution.py:408
  7.0 0.1 broadcast_select_fusion.80
  7.1 0.7 %collective-permute-start.79 = (bf16[1952,128]{1,0:T(8,128)(2,1)S(1)}, bf16[1952,128]{1,0:T(8,128)(2,1)S(1)}, u32[]{:S(2)}, u32[]{:S(2)}) collective-permute-start(bf16[1952,128]{1,0:T(8,128)(2,1)S(1)} %get-tuple-element.1091), channel_id=1, source_target_pairs={{1,256},{3,258},{5,260},{7,262},{9,264},{11,266},{13,268},{15,270}... | collective-permute-start | bytes 1499144 | tf_op jit(solution)/shard_map/cond/branch_45_fun/ppermute | solution.py:400
  7.8 1.3 %collective-permute-start.80 = (bf16[1952,128]{1,0:T(8,128)(2,1)S(1)}, bf16[1952,128]{1,0:T(8,128)(2,1)S(1)}, u32[]{:S(2)}, u32[]{:S(2)}) collective-permute-start(bf16[1952,128]{1,0:T(8,128)(2,1)S(1)} %get-tuple-element.1090), channel_id=1, source_target_pairs={{256,0},{258,2},{260,4},{262,6},{264,8},{266,10},{268,12},{270,14}... | collective-permute-start | bytes 1499144 | tf_op jit(solution)/shard_map/cond/branch_45_fun/ppermute | solution.py:400
  9.1 7.2 %collective-permute-start.81 = (bf16[1952,128]{1,0:T(8,128)(2,1)S(1)}, bf16[1952,128]{1,0:T(8,128)(2,1)S(1)}, u32[]{:S(2)}, u32[]{:S(2)}) collective-permute-start(bf16[1952,128]{1,0:T(8,128)(2,1)S(1)} %get-tuple-element.1089), channel_id=1, source_target_pairs={{0,1},{2,3},{4,5},{6,7},{8,9},{10,11},{12,13},{14,15},{16,17},{18,... | collective-permute-start | bytes 1499144 | tf_op jit(solution)/shard_map/cond/branch_45_fun/ppermute | solution.py:400
  16.3 0.0 collective-permute-done.79
  16.3 16.9 %collective-permute-done.80 = bf16[1952,128]{1,0:T(8,128)(2,1)S(1)} collective-permute-done((bf16[1952,128]{1,0:T(8,128)(2,1)S(1)}, bf16[1952,128]{1,0:T(8,128)(2,1)S(1)}, u32[]{:S(2)}, u32[]{:S(2)}) %collective-permute-start.80) | collective-permute-done | bytes 499744 | tf_op jit(solution)/shard_map/cond/branch_45_fun/ppermute | solution.py:400
  33.3 0.0 collective-permute-done.81
  33.3 0.2 select_select_fusion.44
  33.7 3.4 %finish_rows.1 = (bf16[128,3584]{1,0:T(8,128)(2,1)}, bf16[128,3584]{1,0:T(8,128)(2,1)}, bf16[128,512]{1,0:T(8,128)(2,1)}, bf16[128,512]{1,0:T(8,128)(2,1)}) custom-call(s32[5,1,128]{2,1,0:T(1,128)S(1)} %get-tuple-element.837.facts_ref, bf16[1952,128]{1,0:T(8,128)(2,1)S(1)} %get-tuple-element.1212.pack, bf16[128,3584]{1,0:T(8,128)(2,1)} %q_hbm.3, ...), custom_call_target="tpu_custom_call" | custom-call | flops 704643072 | bytes 4194304 | tf_op jit(solution)/shard_map/finish_rows/pallas_call | solution.py:349
  (2 shorter events, 0.0 us)
Async XLA Ops:
  3.2 3.8 %collective-permute-start.117 = (bf16[1952,128]{1,0:T(8,128)(2,1)S(1)}, bf16[1952,128]{1,0:T(8,128)(2,1)S(1)}, u32[]{:S(2)}, u32[]{:S(2)}) collective-permute-start(bf16[1952,128]{1,0:T(8,128)(2,1)S(1)} %get-tuple-element.838), channel_id=1, source_target_pairs={{0,8},{8,0},{16,24},{24,16},{32,40},{40,32},{48,56},{56,48},{64,72... | collective-permute-start | bytes 1499144 | tf_op jit(solution)/shard_map/ppermute | solution.py:381
  7.1 9.2 %collective-permute-start.79 = (bf16[1952,128]{1,0:T(8,128)(2,1)S(1)}, bf16[1952,128]{1,0:T(8,128)(2,1)S(1)}, u32[]{:S(2)}, u32[]{:S(2)}) collective-permute-start(bf16[1952,128]{1,0:T(8,128)(2,1)S(1)} %get-tuple-element.1091), channel_id=1, source_target_pairs={{1,256},{3,258},{5,260},{7,262},{9,264},{11,266},{13,268},{15,270}... | collective-permute-start | bytes 1499144 | tf_op jit(solution)/shard_map/cond/branch_45_fun/ppermute | solution.py:400
  7.8 25.4 %collective-permute-start.80 = (bf16[1952,128]{1,0:T(8,128)(2,1)S(1)}, bf16[1952,128]{1,0:T(8,128)(2,1)S(1)}, u32[]{:S(2)}, u32[]{:S(2)}) collective-permute-start(bf16[1952,128]{1,0:T(8,128)(2,1)S(1)} %get-tuple-element.1090), channel_id=1, source_target_pairs={{256,0},{258,2},{260,4},{262,6},{264,8},{266,10},{268,12},{270,14}... | collective-permute-start | bytes 1499144 | tf_op jit(solution)/shard_map/cond/branch_45_fun/ppermute | solution.py:400
  9.1 24.1 %collective-permute-start.81 = (bf16[1952,128]{1,0:T(8,128)(2,1)S(1)}, bf16[1952,128]{1,0:T(8,128)(2,1)S(1)}, u32[]{:S(2)}, u32[]{:S(2)}) collective-permute-start(bf16[1952,128]{1,0:T(8,128)(2,1)S(1)} %get-tuple-element.1089), channel_id=1, source_target_pairs={{0,1},{2,3},{4,5},{6,7},{8,9},{10,11},{12,13},{14,15},{16,17},{18,... | collective-permute-start | bytes 1499144 | tf_op jit(solution)/shard_map/cond/branch_45_fun/ppermute | solution.py:400
